TPU v7x, 256 devices: a whole 4x4x8 slice. The times are simulated.
256 devices in a mesh: leaf: 32 (over x, y, core), sep: 8 (over z).
Axes of the slice: x: 4, y: 4, z: 8, core: 2. Of those that a mesh axis runs over, the one named last changes fastest.
Arguments:
- leaf_rhs: bfloat16 [64, 32, 8, 256], P(None, 'leaf', 'sep'), may hold values from -6 to 6
- leaf_inv: bfloat16 [32, 8, 256, 256], P('leaf', 'sep'), as said below
- leaf_coupling: bfloat16 [32, 8, 256, 16128], P('leaf', 'sep')
- block_mask: int32 [32, 8, 126], P('leaf', 'sep'), may hold values 0 or 1
- leaf_rows: int32 [32, 8], P('leaf', 'sep'), may hold values from 1 to 256, 1280 in all within a row
- sep_rhs: bfloat16 [64, 32, 8, 192], P(None, 'leaf', 'sep'), may hold values from -6 to 6
- dinv_rows: float32 [32, 8, 32, 16128], P('leaf', 'sep'), as said below
- sep_coupling: float32 [32, 8, 32, 15872], P('leaf', 'sep')
Outputs:
- leaf_solution: bfloat16 [64, 32, 8, 256], P(None, 'leaf', 'sep')
- sep_solution: float32 [64, 32, 8, 192], P(None, 'leaf', 'sep')
Inputs may be any that keep to these rules, and one draw needn't show every extreme that they name: leaf_inv[l, s, k, j] is 0 for k > j, and its diagonal lies in 0.6 to 1.6. dinv_rows holds rows of lower triangular matrices: entry (g, g') of a separator's block is 0 for g' > g, and its diagonal lies in 0.7 to 1.5.
All inputs are finite; a program needn't handle non-finite values. No bound on the sum of `block_mask` or of `leaf_rows` on one device may be relied on, other than what follows from the above.
Results may differ from a plain program's by a relative error of at most 0.0017.
Values sent between devices are 32-bit elements; how exact they have to be, the bound alone decides.
A program may use at most 64 MiB of HBM per device.

v0:
```python
import jax
import jax.numpy as jnp
from jax import lax
from jax.sharding import PartitionSpec as P


def swapped(shard, axis, stride):
    return lax.ppermute(shard, axis, [(i, i ^ 1 << stride) for i in range(lax.axis_size(axis))])


def body(
    leaf_rhs, leaf_inv, leaf_coupling, block_mask, leaf_rows, sep_rhs, dinv_rows, sep_coupling
):
    leaf_count = lax.axis_size("leaf")
    sep_count = lax.axis_size("sep")
    levels = leaf_count.bit_length()
    leaf_index = lax.axis_index("leaf")
    sep_index = lax.axis_index("sep")
    right_side = leaf_rhs[:, 0, 0, :]
    leaf_width = right_side.shape[1]
    live_rows = jnp.arange(leaf_width, dtype=jnp.int32) < leaf_rows[0, 0]
    right_side = jnp.where(live_rows[None, :], right_side, jnp.zeros_like(right_side))
    solved = jnp.dot(right_side, leaf_inv[0, 0], preferred_element_type=jnp.float32)
    leaf_solution = jnp.where(live_rows[None, :], solved, 0.0).astype(jnp.bfloat16)
    terms = jnp.dot(leaf_solution, leaf_coupling[0, 0], preferred_element_type=jnp.float32)
    block_count = block_mask.shape[2]
    rhs_count = terms.shape[0]
    terms = terms.reshape(rhs_count, block_count, terms.shape[1] // block_count)
    terms = (terms * block_mask[0, 0].astype(jnp.float32)[None, :, None]).reshape(rhs_count, -1)
    per_sep = sep_rhs.shape[3] // levels
    base_rows = per_sep * sep_count
    outputs = []
    carried = None
    for level_idx in range(levels):
        members = 2**level_idx
        seg_width = base_rows * members
        offset = base_rows * (members - 1)
        member = leaf_index % members
        partial_value = -terms[:, offset : offset + seg_width]
        if carried is not None:
            partial_value = partial_value - carried
        own_rows = sep_rhs[:, 0, 0, level_idx * per_sep : (level_idx + 1) * per_sep].astype(
            jnp.float32
        )
        row_start = (member * sep_count + sep_index) * per_sep
        current = lax.dynamic_slice_in_dim(partial_value, row_start, per_sep, 1)
        partial_value = lax.dynamic_update_slice_in_dim(
            partial_value, current + own_rows, row_start, 1
        )
        summed = partial_value
        for bit_pos in range(level_idx):
            summed = summed + swapped(summed, "leaf", bit_pos)
        summed = lax.psum(summed, "sep")
        inverse = dinv_rows[0, 0, :, offset : offset + seg_width]
        solved_sep = lax.dot_general(
            summed,
            inverse,
            (((1,), (1,)), ((), ())),
            precision=lax.Precision.HIGHEST,
            preferred_element_type=jnp.float32,
        )
        outputs.append(solved_sep)
        if level_idx < levels - 1:
            parent_start = base_rows * (2 * members - 2)
            couple = sep_coupling[0, 0, :, parent_start : parent_start + 2 * seg_width]
            carried = jnp.dot(
                solved_sep,
                couple,
                precision=lax.Precision.HIGHEST,
                preferred_element_type=jnp.float32,
            )
    sep_solution = jnp.concatenate(outputs, axis=1)
    return (leaf_solution[:, None, None, :], sep_solution[:, None, None, :])


def solution(mesh):
    return jax.shard_map(
        body,
        mesh=mesh,
        in_specs=(
            P(None, "leaf", "sep", None),
            P("leaf", "sep", None, None),
            P("leaf", "sep", None, None),
            P("leaf", "sep", None),
            P("leaf", "sep"),
            P(None, "leaf", "sep", None),
            P("leaf", "sep", None, None),
            P("leaf", "sep", None, None),
        ),
        out_specs=(P(None, "leaf", "sep", None), P(None, "leaf", "sep", None)),
        check_vma=False,
    )
```

profile of v0, /device:TPU:1, one launch (start us, length us, event | category | flops | bytes accessed | tf_op | source)
XLA Modules:
  0.0 821.6 jit_solution(18331422370298422273)
XLA Ops:
  7.9 11.8 %copy.12 = bf16[1,1,256,16128]{2,3,1,0:T(8,128)(2,1)} copy(bf16[1,1,256,16128]{3,2,1,0:T(8,128)(2,1)} %param.10) | data formatting | bytes 16515072 | tf_op args[2]
  19.9 6.0 multiply_bitcast_fusion
  25.9 0.3 copy.17
  26.2 1.9 copy-done.2
  28.2 0.4 dynamic_update_slice.18
  28.6 0.6 copy-done.4
  29.3 70.1 %all-reduce.7.cloned.1.call-done = f32[64,256]{1,0:T(8,128)} async-done(((f32[64,256]{1,0:T(8,128)}), f32[64,256]{1,0:T(8,128)}) %all-reduce.7.cloned.1.call-update) | async-done | bytes 65552 | tf_op jit(solution)/shard_map/psum | solution.py:53
  99.5 1.0 constant_dynamic-update-slice_fusion.4
  100.5 1.3 convolution_subtract_fusion.4
  101.9 0.4 dynamic_update_slice.19
  102.3 5.7 collective-permute-start
  108.0 1.0 collective-permute-done
  109.0 0.7 add.138
  109.7 65.2 %all-reduce.9.cloned.1.call-done = f32[64,512]{1,0:T(8,128)} async-done(((f32[64,512]{1,0:T(8,128)}), f32[64,512]{1,0:T(8,128)}) %all-reduce.9.cloned.1.call-update) | async-done | bytes 131088 | tf_op jit(solution)/shard_map/psum | solution.py:53
  175.0 1.1 constant_dynamic-update-slice_fusion.3
  176.1 1.4 convolution_subtract_fusion.3
  177.7 0.4 dynamic_update_slice.20
  178.1 5.8 collective-permute-start.1
  183.9 1.2 collective-permute-done.1
  185.1 1.3 collective-permute-start.2
  186.4 6.3 collective-permute-done.2
  192.7 0.7 add.144
  193.5 67.1 %all-reduce.11.cloned.1.call-done = f32[64,1024]{1,0:T(8,128)} async-done(((f32[64,1024]{1,0:T(8,128)}), f32[64,1024]{1,0:T(8,128)}) %all-reduce.11.cloned.1.call-update) | async-done | bytes 262160 | tf_op jit(solution)/shard_map/psum | solution.py:53
  260.6 1.3 constant_dynamic-update-slice_fusion.2
  262.0 1.8 convolution_subtract_fusion.2
  263.8 0.4 dynamic_update_slice.21
  264.3 5.3 collective-permute-start.3
  269.5 1.5 collective-permute-done.3
  271.2 1.3 collective-permute-start.4
  272.5 11.9 %collective-permute-done.4 = f32[64,2048]{1,0:T(8,128)S(1)} collective-permute-done((f32[64,2048]{1,0:T(8,128)S(1)}, f32[64,2048]{1,0:T(8,128)S(1)}, u32[]{:S(2)}, u32[]{:S(2)}) %collective-permute-start.4) | collective-permute-done | bytes 524320 | tf_op jit(solution)/shard_map/ppermute | solution.py:8
  284.4 2.8 collective-permute-start.5
  287.3 11.0 %collective-permute-done.5 = f32[64,2048]{1,0:T(8,128)S(1)} collective-permute-done((f32[64,2048]{1,0:T(8,128)S(1)}, f32[64,2048]{1,0:T(8,128)S(1)}, u32[]{:S(2)}, u32[]{:S(2)}) %collective-permute-start.5) | collective-permute-done | bytes 524320 | tf_op jit(solution)/shard_map/ppermute | solution.py:8
  298.3 0.9 add.151
  299.2 68.9 %all-reduce.13.cloned.1.call-done = f32[64,2048]{1,0:T(8,128)} async-done(((f32[64,2048]{1,0:T(8,128)}), f32[64,2048]{1,0:T(8,128)}) %all-reduce.13.cloned.1.call-update) | async-done | bytes 524304 | tf_op jit(solution)/shard_map/psum | solution.py:53
  368.1 1.6 constant_dynamic-update-slice_fusion.1
  369.7 2.4 convolution_subtract_fusion.1
  372.2 0.4 dynamic_update_slice.22
  372.7 5.3 collective-permute-start.6
  378.0 2.3 collective-permute-done.6
  380.4 1.3 collective-permute-start.7
  381.7 23.2 %collective-permute-done.7 = f32[64,4096]{1,0:T(8,128)S(1)} collective-permute-done((f32[64,4096]{1,0:T(8,128)S(1)}, f32[64,4096]{1,0:T(8,128)S(1)}, u32[]{:S(2)}, u32[]{:S(2)}) %collective-permute-start.7) | collective-permute-done | bytes 1048608 | tf_op jit(solution)/shard_map/ppermute | solution.py:8
  404.9 3.0 collective-permute-start.8
  408.0 22.2 %collective-permute-done.8 = f32[64,4096]{1,0:T(8,128)S(1)} collective-permute-done((f32[64,4096]{1,0:T(8,128)S(1)}, f32[64,4096]{1,0:T(8,128)S(1)}, u32[]{:S(2)}, u32[]{:S(2)}) %collective-permute-start.8) | collective-permute-done | bytes 1048608 | tf_op jit(solution)/shard_map/ppermute | solution.py:8
  430.3 1.3 collective-permute-start.9
  431.6 21.3 %collective-permute-done.9 = f32[64,4096]{1,0:T(8,128)S(1)} collective-permute-done((f32[64,4096]{1,0:T(8,128)S(1)}, f32[64,4096]{1,0:T(8,128)S(1)}, u32[]{:S(2)}, u32[]{:S(2)}) %collective-permute-start.9) | collective-permute-done | bytes 1048608 | tf_op jit(solution)/shard_map/ppermute | solution.py:8
  452.9 1.1 add.159
  454.1 72.7 %all-reduce.15.cloned.1.call-done = f32[64,4096]{1,0:T(8,128)} async-done(((f32[64,4096]{1,0:T(8,128)}), f32[64,4096]{1,0:T(8,128)}) %all-reduce.15.cloned.1.call-update) | async-done | bytes 1048592 | tf_op jit(solution)/shard_map/psum | solution.py:53
  526.8 2.3 constant_dynamic-update-slice_fusion
  529.1 3.8 convolution_subtract_fusion
  533.0 0.4 dynamic_update_slice.23
  533.5 5.2 collective-permute-start.10
  538.7 3.8 collective-permute-done.10
  542.7 1.0 collective-permute-start.11
  543.7 46.0 %collective-permute-done.11 = f32[64,8192]{1,0:T(8,128)S(1)} collective-permute-done((f32[64,8192]{1,0:T(8,128)S(1)}, f32[64,8192]{1,0:T(8,128)S(1)}, u32[]{:S(2)}, u32[]{:S(2)}) %collective-permute-start.11) | collective-permute-done | bytes 2097184 | tf_op jit(solution)/shard_map/ppermute | solution.py:8
  589.9 2.5 collective-permute-start.12
  592.4 45.0 %collective-permute-done.12 = f32[64,8192]{1,0:T(8,128)S(1)} collective-permute-done((f32[64,8192]{1,0:T(8,128)S(1)}, f32[64,8192]{1,0:T(8,128)S(1)}, u32[]{:S(2)}, u32[]{:S(2)}) %collective-permute-start.12) | collective-permute-done | bytes 2097184 | tf_op jit(solution)/shard_map/ppermute | solution.py:8
  637.6 0.9 collective-permute-start.13
  638.5 44.1 %collective-permute-done.13 = f32[64,8192]{1,0:T(8,128)S(1)} collective-permute-done((f32[64,8192]{1,0:T(8,128)S(1)}, f32[64,8192]{1,0:T(8,128)S(1)}, u32[]{:S(2)}, u32[]{:S(2)}) %collective-permute-start.13) | collective-permute-done | bytes 2097184 | tf_op jit(solution)/shard_map/ppermute | solution.py:8
  682.9 2.4 collective-permute-start.14
  685.4 43.2 %collective-permute-done.14 = f32[64,8192]{1,0:T(8,128)S(1)} collective-permute-done((f32[64,8192]{1,0:T(8,128)S(1)}, f32[64,8192]{1,0:T(8,128)S(1)}, u32[]{:S(2)}, u32[]{:S(2)}) %collective-permute-start.14) | collective-permute-done | bytes 2097184 | tf_op jit(solution)/shard_map/ppermute | solution.py:8
  728.6 1.5 add.168
  730.1 80.6 %all-reduce.17.cloned.1.call-done = f32[64,8192]{1,0:T(8,128)} async-done(((f32[64,8192]{1,0:T(8,128)}), f32[64,8192]{1,0:T(8,128)}) %all-reduce.17.cloned.1.call-update) | async-done | bytes 2097168 | tf_op jit(solution)/shard_map/psum | solution.py:53
  810.7 3.3 convolution_dynamic-update-slice_fusion
  814.1 0.7 copy.14
  (48 shorter events, 2.4 us)
Async XLA Ops:
  7.2 12.6 %copy-start = (bf16[1,1,256,256]{3,2,1,0:T(8,128)(2,1)S(1)}, bf16[1,1,256,256]{3,2,1,0:T(8,128)(2,1)}, u32[]{:S(2)}) copy-start(bf16[1,1,256,256]{3,2,1,0:T(8,128)(2,1)} %param.9) | copy-start | bytes 393220
  7.2 92.3 %all-reduce.7.cloned.1.call-start = ((), (), s32[]{:S(2)}) async-start(), calls=%async_computation | async-start | bytes 131072 | tf_op jit(solution)/shard_map/psum | solution.py:53
  7.9 11.8 %copy-start.8 = (s32[1,1,126]{2,1,0:T(1,128)S(1)}, s32[1,1,126]{2,1,0:T(1,128)}, u32[]{:S(2)}) copy-start(s32[1,1,126]{2,1,0:T(1,128)} %param.11) | copy-start | bytes 1516
  7.9 11.8 %copy-start.7 = (bf16[64,1,1,256]{3,0,2,1:T(8,128)(2,1)S(1)}, bf16[64,1,1,256]{3,0,2,1:T(8,128)(2,1)}, u32[]{:S(2)}) copy-start(bf16[64,1,1,256]{3,0,2,1:T(8,128)(2,1)} %param.8) | copy-start | bytes 98308
  19.9 6.0 copy-start.6
  25.9 2.2 copy-start.5
  26.2 1.9 copy-start.2
  28.6 0.6 copy-start.4
  29.3 145.7 %all-reduce.9.cloned.1.call-start = ((), (), s32[]{:S(2)}) async-start(), calls=%async_computation.1 | async-start | bytes 262144 | tf_op jit(solution)/shard_map/psum | solution.py:53
  102.3 6.7 collective-permute-start
  109.7 151.0 %all-reduce.11.cloned.1.call-start = ((), (), s32[]{:S(2)}) async-start(), calls=%async_computation.2 | async-start | bytes 524288 | tf_op jit(solution)/shard_map/psum | solution.py:53
  178.1 6.9 collective-permute-start.1
  185.1 7.6 collective-permute-start.2
  193.5 174.6 %all-reduce.13.cloned.1.call-start = ((), (), s32[]{:S(2)}) async-start(), calls=%async_computation.3 | async-start | bytes 1048576 | tf_op jit(solution)/shard_map/psum | solution.py:53
  264.3 6.8 collective-permute-start.3
  271.2 13.2 %collective-permute-start.4 = (f32[64,2048]{1,0:T(8,128)S(1)}, f32[64,2048]{1,0:T(8,128)S(1)}, u32[]{:S(2)}, u32[]{:S(2)}) collective-permute-start(f32[64,2048]{1,0:T(8,128)S(1)} %add.149), channel_id=1, source_target_pairs={{0,16},{8,24},{16,0},{24,8},{32,48},{40,56},{48,32},{56,40},{64,80... | collective-permute-start | bytes 1572872 | tf_op jit(solution)/shard_map/ppermute | solution.py:8
  284.4 13.8 %collective-permute-start.5 = (f32[64,2048]{1,0:T(8,128)S(1)}, f32[64,2048]{1,0:T(8,128)S(1)}, u32[]{:S(2)}, u32[]{:S(2)}) collective-permute-start(f32[64,2048]{1,0:T(8,128)S(1)} %add.150), channel_id=1, source_target_pairs={{0,32},{8,40},{16,48},{24,56},{32,0},{40,8},{48,16},{56,24},{64,96... | collective-permute-start | bytes 1572872 | tf_op jit(solution)/shard_map/ppermute | solution.py:8
  299.1 227.7 %all-reduce.15.cloned.1.call-start = ((), (), s32[]{:S(2)}) async-start(), calls=%async_computation.4 | async-start | bytes 2097152 | tf_op jit(solution)/shard_map/psum | solution.py:53
  372.7 7.6 collective-permute-start.6
  380.4 24.5 %collective-permute-start.7 = (f32[64,4096]{1,0:T(8,128)S(1)}, f32[64,4096]{1,0:T(8,128)S(1)}, u32[]{:S(2)}, u32[]{:S(2)}) collective-permute-start(f32[64,4096]{1,0:T(8,128)S(1)} %add.156), channel_id=1, source_target_pairs={{0,16},{8,24},{16,0},{24,8},{32,48},{40,56},{48,32},{56,40},{64,80... | collective-permute-start | bytes 3145736 | tf_op jit(solution)/shard_map/ppermute | solution.py:8
  404.9 25.2 %collective-permute-start.8 = (f32[64,4096]{1,0:T(8,128)S(1)}, f32[64,4096]{1,0:T(8,128)S(1)}, u32[]{:S(2)}, u32[]{:S(2)}) collective-permute-start(f32[64,4096]{1,0:T(8,128)S(1)} %add.157), channel_id=1, source_target_pairs={{0,32},{8,40},{16,48},{24,56},{32,0},{40,8},{48,16},{56,24},{64,96... | collective-permute-start | bytes 3145736 | tf_op jit(solution)/shard_map/ppermute | solution.py:8
  430.3 22.6 %collective-permute-start.9 = (f32[64,4096]{1,0:T(8,128)S(1)}, f32[64,4096]{1,0:T(8,128)S(1)}, u32[]{:S(2)}, u32[]{:S(2)}) collective-permute-start(f32[64,4096]{1,0:T(8,128)S(1)} %add.158), channel_id=1, source_target_pairs={{0,64},{8,72},{16,80},{24,88},{32,96},{40,104},{48,112},{56,120},{... | collective-permute-start | bytes 3145736 | tf_op jit(solution)/shard_map/ppermute | solution.py:8
  454.0 356.7 %all-reduce.17.cloned.1.call-start = ((), (), s32[]{:S(2)}) async-start(), calls=%async_computation.5 | async-start | bytes 4194304 | tf_op jit(solution)/shard_map/psum | solution.py:53
  533.5 9.0 %collective-permute-start.10 = (f32[64,8192]{1,0:T(8,128)S(1)}, f32[64,8192]{1,0:T(8,128)S(1)}, u32[]{:S(2)}, u32[]{:S(2)}) collective-permute-start(f32[64,8192]{1,0:T(8,128)S(1)} %dynamic_update_slice.23), channel_id=1, source_target_pairs={{0,8},{8,0},{16,24},{24,16},{32,40},{40,32},{48,56},{56,48},{64,72... | collective-permute-start | bytes 6291464 | tf_op jit(solution)/shard_map/ppermute | solution.py:8
  542.7 46.9 %collective-permute-start.11 = (f32[64,8192]{1,0:T(8,128)S(1)}, f32[64,8192]{1,0:T(8,128)S(1)}, u32[]{:S(2)}, u32[]{:S(2)}) collective-permute-start(f32[64,8192]{1,0:T(8,128)S(1)} %add.164), channel_id=1, source_target_pairs={{0,16},{8,24},{16,0},{24,8},{32,48},{40,56},{48,32},{56,40},{64,80... | collective-permute-start | bytes 6291464 | tf_op jit(solution)/shard_map/ppermute | solution.py:8
  589.9 47.5 %collective-permute-start.12 = (f32[64,8192]{1,0:T(8,128)S(1)}, f32[64,8192]{1,0:T(8,128)S(1)}, u32[]{:S(2)}, u32[]{:S(2)}) collective-permute-start(f32[64,8192]{1,0:T(8,128)S(1)} %add.165), channel_id=1, source_target_pairs={{0,32},{8,40},{16,48},{24,56},{32,0},{40,8},{48,16},{56,24},{64,96... | collective-permute-start | bytes 6291464 | tf_op jit(solution)/shard_map/ppermute | solution.py:8
  637.6 45.1 %collective-permute-start.13 = (f32[64,8192]{1,0:T(8,128)S(1)}, f32[64,8192]{1,0:T(8,128)S(1)}, u32[]{:S(2)}, u32[]{:S(2)}) collective-permute-start(f32[64,8192]{1,0:T(8,128)S(1)} %add.166), channel_id=1, source_target_pairs={{0,64},{8,72},{16,80},{24,88},{32,96},{40,104},{48,112},{56,120},{... | collective-permute-start | bytes 6291464 | tf_op jit(solution)/shard_map/ppermute | solution.py:8
  682.9 45.7 %collective-permute-start.14 = (f32[64,8192]{1,0:T(8,128)S(1)}, f32[64,8192]{1,0:T(8,128)S(1)}, u32[]{:S(2)}, u32[]{:S(2)}) collective-permute-start(f32[64,8192]{1,0:T(8,128)S(1)} %add.167), channel_id=1, source_target_pairs={{0,128},{8,136},{16,144},{24,152},{32,160},{40,168},{48,176},{56,1... | collective-permute-start | bytes 6291464 | tf_op jit(solution)/shard_map/ppermute | solution.py:8
  730.1 80.6 %copy-start.3 = (f32[1,1,32,16128]{3,2,1,0:T(8,128)S(1)}, f32[1,1,32,16128]{3,2,1,0:T(8,128)}, u32[]{:S(2)}) copy-start(f32[1,1,32,16128]{3,2,1,0:T(8,128)} %param.14) | copy-start | bytes 6193156
  730.1 84.7 %copy-start.1 = (bf16[1,1,256,256]{3,2,1,0:T(8,128)(2,1)S(1)}, bf16[1,1,256,256]{3,2,1,0:T(8,128)(2,1)}, u32[]{:S(2)}) copy-start(bf16[1,1,256,256]{3,2,1,0:T(8,128)(2,1)} %param.9) | copy-start | bytes 393220
Sparse Core Ops, SparseCore 0:
  29.4 70.0 all-reduce.6
  109.8 65.1 all-reduce.8
  193.6 67.0 all-reduce.10
  299.3 68.7 all-reduce.12
  454.1 72.6 all-reduce.14
  730.2 80.4 all-reduce.16
where the time goes:
time: 824 us; the launch traced here: 822 us
  waiting for transfers between devices  709 us (86%)
  starting transfers between devices  45.3 us (5%)
  matrix products  27.6 us (3%)
  local copies, waits for them, and re-layouts  18 us (2%)
  between operations  15.2 us (2%)
    psum x6, waiting for transfers between devices, body(): summed = lax.psum(summed, 'sep')  425 us
    ppermute x15, waiting for transfers between devices, swapped(): lax.ppermute(shard, axis, [(i, i ^ 1 << stride) for i in range(lax.axis_s...  284 us
    ppermute x15, starting transfers between devices, swapped(): lax.ppermute(shard, axis, [(i, i ^ 1 << stride) for i in range(lax.axis_s...  45 us
  transfers between devices with their start and end apart: 21, of which 21 were waited for; matrix products, arithmetic and copies ran while one was open for 0% of the time, Pallas kernels for 0%

commit v1 on v0

v1 whole, which is shorter than its diff:
```python
import functools

import jax
import jax.numpy as jnp
from jax import lax
from jax.experimental import pallas as pl
from jax.experimental.pallas import tpu as pltpu
from jax.sharding import PartitionSpec as P

MESH = pl.DeviceIdType.MESH
LEVELS = 6
SEPS = 8
RHS = 64
CH = 256
F32 = jnp.float32
BF16 = jnp.bfloat16


def first_chunk(v):
    return 2**v - 1


def xy_slot(v):
    return sum(2 ** (u - 1) - 1 for u in range(2, v))


def core_slot(v):
    return 2 ** (v - 1) - 1


def split(x):
    hi = x.astype(BF16)
    lo = (x - hi.astype(F32)).astype(BF16)
    return hi, lo


def kernel(
    mask_ref, rows_ref, rhs_ref, inv_ref, srhs_ref, coup_hbm, dinv_hbm, scoup_hbm,
    leaf_out, sep_out,
    weights, dfull, cfull, dstack, cstack, part, core_in, xy_in, z_out, z_in, resid, sol_ref,
    sem_w, sem_d, sem_c,
    zr_s, zr_r, zg_s, zg_r, xr_s, xr_r, xg_s, xg_r, cr_s, cr_r, cg_s, cg_r,
):
    leaf = lax.axis_index("leaf")
    sep = lax.axis_index("sep")
    core = lax.rem(leaf, 2)
    other = 1 - core
    bits = [lax.rem(leaf // 2 ** (k + 1), 2) for k in range(4)]
    partner = leaf + 1 - 2 * core

    def xy_of(v):
        return lax.rem(leaf // 2, 2 ** (v - 1))

    def flip(d):
        return sum(2**k * (1 - 2 * bits[k]) for k in range(4) if d >> k & 1)

    def place(v, which_core, xy):
        if v == 0:
            return 0
        return first_chunk(v) + which_core * 2 ** (v - 1) + xy

    def mine(v):
        return 0 if v == 0 else place(v, core, xy_of(v))

    def column(v, which_core, xy):
        if v == 0:
            return 0
        return pl.multiple_of((first_chunk(v) + 2 * xy + which_core) * CH, CH)

    def peers(v):
        return range(1, 2 ** (v - 1)) if v >= 2 else range(0)

    def level_cols(v):
        return pl.ds(first_chunk(v) * CH, 2**v * CH)

    def parent_cols(v):
        return pl.ds((first_chunk(v) - 1) * CH, 2**v * CH)

    def load_w(v):
        return pltpu.make_async_copy(
            coup_hbm.at[:, level_cols(v)], weights.at[:, level_cols(v)], sem_w.at[v])

    def load_d(v):
        return pltpu.make_async_copy(
            dinv_hbm.at[:, level_cols(v)], dfull.at[:, level_cols(v)], sem_d.at[v])

    def load_c(v):
        return pltpu.make_async_copy(
            scoup_hbm.at[:, parent_cols(v)], cfull.at[:, parent_cols(v)], sem_c.at[v])

    def remote(src, dst, send, recv, to):
        return pltpu.make_async_remote_copy(
            src_ref=src, dst_ref=dst, send_sem=send, recv_sem=recv,
            device_id=to, device_id_type=MESH)

    def z_peer(d):
        return lax.rem(sep + d, SEPS)

    def zr(v, d):
        return remote(z_out.at[v, z_peer(d)], z_in.at[v, d - 1],
                      zr_s.at[v, d - 1], zr_r.at[v, d - 1], (leaf, z_peer(d)))

    def zg(v, d):
        return remote(resid.at[mine(v), sep], resid.at[mine(v), sep],
                      zg_s.at[v, d - 1], zg_r.at[v, d - 1], (leaf, z_peer(d)))

    def zg_in(v, d):
        src = z_peer(SEPS - d)
        return remote(resid.at[mine(v), src], resid.at[mine(v), src],
                      zg_s.at[v, d - 1], zg_r.at[v, d - 1], (leaf, z_peer(d)))

    def xr(v, d):
        k = xy_slot(v) + d - 1
        return remote(part.at[place(v, core, xy_of(v) + flip(d))], xy_in.at[k],
                      xr_s.at[k], xr_r.at[k], (leaf + 2 * flip(d), sep))

    def xg(v, d, incoming=False):
        k = xy_slot(v) + d - 1
        at = place(v, core, xy_of(v) + (flip(d) if incoming else 0))
        return remote(resid.at[at], resid.at[at],
                      xg_s.at[k], xg_r.at[k], (leaf + 2 * flip(d), sep))

    def cr(v, i):
        k = core_slot(v) + i
        return remote(part.at[place(v, other, i)], core_in.at[k],
                      cr_s.at[k], cr_r.at[k], (partner, sep))

    def cg(v, d, incoming=False):
        k = core_slot(v) + d
        at = place(v, other if incoming else core, xy_of(v) + flip(d))
        return remote(resid.at[at], resid.at[at],
                      cg_s.at[k], cg_r.at[k], (partner, sep))

    for v in range(LEVELS):
        load_w(v).start()
        load_d(v).start()
        if v:
            load_c(v).start()

    barrier = pltpu.get_barrier_semaphore()
    pl.semaphore_signal(barrier, inc=1, device_id=(partner, sep), device_id_type=MESH)
    for d in range(1, 16):
        pl.semaphore_signal(
            barrier, inc=1, device_id=(leaf + 2 * flip(d), sep), device_id_type=MESH)
    for d in range(1, SEPS):
        pl.semaphore_signal(
            barrier, inc=1, device_id=(leaf, z_peer(d)), device_id_type=MESH)

    live = lax.broadcasted_iota(jnp.int32, (RHS, CH), 1) < rows_ref[0, 0]
    right = jnp.where(live, rhs_ref[...].astype(F32), 0.0).astype(BF16)
    solved = jnp.dot(right, inv_ref[...], preferred_element_type=F32)
    solved = jnp.where(live, solved, 0.0).astype(BF16)
    sol_ref[...] = solved
    leaf_out[...] = solved

    def terms_chunk(v, which_core, xy):
        m = 0 if v == 0 else 2 * xy + which_core
        block = 2 * (first_chunk(v) + m)
        col = column(v, which_core, xy)
        t = jnp.dot(sol_ref[...], weights[:, pl.ds(col, CH)], preferred_element_type=F32)
        left = t[:, :128] * (-mask_ref[block].astype(F32))
        rest = t[:, 128:] * (-mask_ref[block + 1].astype(F32))
        t = jnp.concatenate([left, rest], axis=1)
        part[place(v, which_core, xy)] = t.reshape(SEPS, 8, CH)

    def terms(v):
        load_w(v).wait()
        if v == 0:
            terms_chunk(0, 0, 0)
        else:
            n = 2 ** (v - 1)
            step = min(n, 2)

            def some(i, carry):
                for j in range(step):
                    for c in range(2):
                        terms_chunk(v, c, i * step + j)
                return carry

            if n == step:
                some(0, 0)
            else:
                lax.fori_loop(0, n // step, some, 0)
        r = lax.broadcasted_iota(jnp.int32, (LEVELS * 32, CH), 0)
        c = lax.broadcasted_iota(jnp.int32, (LEVELS * 32, CH), 1)
        pick = jnp.where((r - 32 * v == c - 32 * sep) & (r >= 32 * v) & (r < 32 * v + 32), 1.0, 0.0)
        own = jnp.dot(srhs_ref[...], pick.astype(BF16), preferred_element_type=F32)
        at = mine(v)
        part[at] = part[at] + own.reshape(SEPS, 8, CH)

    def stack(src, dst, start, size):
        cols = pl.ds(pl.multiple_of(start, CH), size)
        hi, lo = split(src[:, cols])
        dst[0:32, cols] = hi
        dst[32:64, cols] = lo
        dst[64:96, cols] = hi
        dst[96:128, cols] = lo

    def stack_all(src, dst, start, size):
        width = min(size, 512)
        if size == width:
            stack(src, dst, start, size)
        else:
            def some(i, carry):
                stack(src, dst, start + i * width, width)
                return carry
            lax.fori_loop(0, size // width, some, 0)

    def prep(v):
        load_d(v).wait()
        stack_all(dfull, dstack, first_chunk(v) * CH, 2**v * CH)
        if v:
            load_c(v).wait()
            stack_all(cfull, cstack, (first_chunk(v) - 1) * CH, 2**v * CH)

    lanes = lax.broadcasted_iota(jnp.int32, (RHS, 128), 1)

    def product(v, which_core, xy, at, acc):
        hi, lo = split(resid[at].reshape(RHS, CH))
        rows = jnp.concatenate([hi, lo], axis=0)
        col = column(v, which_core, xy)
        return acc + lax.dot_general(
            rows, dstack[:, pl.ds(col, CH)], (((1,), (1,)), ((), ())),
            preferred_element_type=F32)

    def couple_chunk(v, xs, which_core, xy):
        at = place(v, which_core, xy)
        col = (first_chunk(v) - 1 + 2 * xy + which_core) * CH
        t = jnp.dot(xs, cstack[:, pl.ds(pl.multiple_of(col, CH), CH)], preferred_element_type=F32)
        part[at] = part[at] - t.reshape(SEPS, 8, CH)

    terms(0)
    z_out[0] = part[0]
    pl.semaphore_wait(barrier, 1 + 15 + 7)

    for v in range(LEVELS):
        if v >= 1:
            n = 2 ** (v - 1)
            step = min(n, 4)

            def theirs(i, carry):
                for j in range(step):
                    couple_chunk(v, xs, other, i * step + j)
                    cr(v, i * step + j).start()
                return carry

            def ours(i, carry):
                for j in range(step):
                    couple_chunk(v, xs, core, i * step + j)
                return carry

            if n == step:
                theirs(0, 0)
                ours(0, 0)
            else:
                lax.fori_loop(0, n // step, theirs, 0)
                lax.fori_loop(0, n // step, ours, 0)
            for d in peers(v):
                i = xy_of(v) + flip(d)
                cr(v, i).wait_recv()
                at = place(v, core, i)
                part[at] = part[at] + core_in[core_slot(v) + i]
                xr(v, d).start()
            i = xy_of(v)
            cr(v, i).wait_recv()
            total = part[mine(v)] + core_in[core_slot(v) + i]
            for d in peers(v):
                xr(v, d).wait_recv()
                total = total + xy_in[xy_slot(v) + d - 1]
            z_out[v] = total
        for d in range(1, SEPS):
            zr(v, d).start()
        if v == 0:
            prep(0)
            terms(1)
            prep(1)
            terms(2)
        elif v < LEVELS - 1:
            prep(v + 1)
        if v >= 1:
            for i in range(2 ** (v - 1)):
                cr(v, i).wait_send()
            for d in peers(v):
                xr(v, d).wait_send()
        total = z_out[v, sep]
        for d in range(1, SEPS):
            zr(v, d).wait_recv()
            total = total + z_in[v, d - 1]
        resid[mine(v), sep] = total
        for d in range(1, SEPS):
            zg(v, d).start()
        if v + 3 < LEVELS:
            terms(v + 3)
        for d in range(1, SEPS):
            zr(v, d).wait_send()
        for d in range(1, SEPS):
            zg_in(v, d).wait_recv()
        if v >= 1:
            cg(v, 0).start()
            for d in peers(v):
                xg(v, d).start()
        acc = jnp.zeros((2 * RHS, 128), F32)
        if v == 0:
            acc = product(0, 0, 0, 0, acc)
        else:
            acc = product(v, core, xy_of(v), mine(v), acc)
            for d in peers(v):
                xg(v, d, True).wait_recv()
                cg(v, d).start()
                i = xy_of(v) + flip(d)
                acc = product(v, core, i, place(v, core, i), acc)
            for d in range(2 ** (v - 1)):
                cg(v, d, True).wait_recv()
                i = xy_of(v) + flip(d)
                acc = product(v, other, i, place(v, other, i), acc)
        t = acc[:RHS] + acc[RHS:]
        x = t + pltpu.roll(t, 32, 1)
        if v < 4:
            old = jnp.zeros_like(x) if v == 0 else sep_out[:, :128]
            sep_out[:, :128] = jnp.where(lanes // 32 == v, x, old)
        else:
            sep_out[:, 32 * v : 32 * v + 32] = x[:, 32 * (v - 4) : 32 * (v - 3)]
        hi, lo = split(x)
        xs = jnp.where(lanes < 64, hi.astype(F32), lo.astype(F32)).astype(BF16)
        for d in range(1, SEPS):
            zg(v, d).wait_send()
        if v >= 1:
            for d in range(2 ** (v - 1)):
                cg(v, d).wait_send()
            for d in peers(v):
                xg(v, d).wait_send()


def body(
    leaf_rhs, leaf_inv, leaf_coupling, block_mask, leaf_rows, sep_rhs, dinv_rows, sep_coupling
):
    sums = leaf_coupling.shape[3]
    parents = sep_coupling.shape[3]
    dma = pltpu.SemaphoreType.DMA
    vmem = pl.BlockSpec(memory_space=pltpu.VMEM)
    smem = pl.BlockSpec(memory_space=pltpu.SMEM)
    hbm = pl.BlockSpec(memory_space=pl.ANY)
    leaf_solution, sep_solution = pl.pallas_call(
        kernel,
        out_shape=(
            jax.ShapeDtypeStruct((RHS, CH), BF16),
            jax.ShapeDtypeStruct((RHS, LEVELS * 32), F32),
        ),
        in_specs=[smem, smem, vmem, vmem, vmem, hbm, hbm, hbm],
        out_specs=(vmem, vmem),
        scratch_shapes=[
            pltpu.VMEM((CH, sums), BF16),
            pltpu.VMEM((32, sums), F32),
            pltpu.VMEM((32, parents), F32),
            pltpu.VMEM((128, sums), BF16),
            pltpu.VMEM((128, parents), BF16),
            pltpu.VMEM((63, SEPS, 8, CH), F32),
            pltpu.VMEM((31, SEPS, 8, CH), F32),
            pltpu.VMEM((26, SEPS, 8, CH), F32),
            pltpu.VMEM((LEVELS, SEPS, 8, CH), F32),
            pltpu.VMEM((LEVELS, SEPS - 1, 8, CH), F32),
            pltpu.VMEM((63, SEPS, 8, CH), F32),
            pltpu.VMEM((RHS, CH), BF16),
            dma((LEVELS,)), dma((LEVELS,)), dma((LEVELS,)),
            dma((LEVELS, 7)), dma((LEVELS, 7)), dma((LEVELS, 7)), dma((LEVELS, 7)),
            dma((26,)), dma((26,)), dma((26,)), dma((26,)),
            dma((31,)), dma((31,)), dma((31,)), dma((31,)),
        ],
        compiler_params=pltpu.CompilerParams(
            collective_id=0, has_side_effects=True, vmem_limit_bytes=60 * 2**20),
        name="forward_substitution",
    )(
        block_mask[0, 0], leaf_rows, leaf_rhs[:, 0, 0, :], leaf_inv[0, 0], sep_rhs[:, 0, 0, :],
        leaf_coupling[0, 0], dinv_rows[0, 0], sep_coupling[0, 0],
    )
    return (leaf_solution[:, None, None, :], sep_solution[:, None, None, :])


def solution(mesh):
    return jax.shard_map(
        body,
        mesh=mesh,
        in_specs=(
            P(None, "leaf", "sep", None),
            P("leaf", "sep", None, None),
            P("leaf", "sep", None, None),
            P("leaf", "sep", None),
            P("leaf", "sep"),
            P(None, "leaf", "sep", None),
            P("leaf", "sep", None, None),
            P("leaf", "sep", None, None),
        ),
        out_specs=(P(None, "leaf", "sep", None), P(None, "leaf", "sep", None)),
        check_vma=False,
    )
```

time: 824 us -> 160 us (0.19)
  waiting for transfers between devices: 709 us -> 0 us
  Pallas kernels: 0 us -> 156 us
  starting transfers between devices: 45.3 us -> 0 us
  matrix products: 27.6 us -> 0 us
  local copies, waits for them, and re-layouts: 18 us -> 2.91 us
  between operations: 15.2 us -> 1.29 us
    psum x6 -> x0, waiting for transfers between devices: 425 us -> none  [body(): summed = lax.psum(summed, 'sep')]
    ppermute x15 -> x0, waiting for transfers between devices: 284 us -> none  [swapped(): lax.ppermute(shard, axis, [(i, i ^ 1 << stride) for i in range(lax.axis_s...]
    pallas_call x0 -> x1, Pallas kernels: none -> 156 us  [body(): pl.pallas_call(kernel, out_shape=(jax.ShapeDtypeStruct((RHS, CH), BF16),...]
    ppermute x15 -> x0, starting transfers between devices: 45 us -> none  [swapped(): lax.ppermute(shard, axis, [(i, i ^ 1 << stride) for i in range(lax.axis_s...]
    dot_general x13 -> x0, matrix products: 27.6 us -> none  [the longest x6 10.7 us: body(): lax.dot_general(summed, inverse, (((1,), (1,)), ((), ())), precision=lax....]
    unnamed x20 -> x2, local copies, waits for them, and re-layouts: 15.1 us -> 2.91 us
  transfers between devices with their start and end apart: 21 -> 0, of which waited for: 21 -> 0; matrix products, arithmetic and copies ran while one was open for 0% -> 0% of each run, Pallas kernels for 0% -> 0%
where the time goes in v1:
time: 160 us
  Pallas kernels  156 us (98%)
  local copies, waits for them, and re-layouts  2.91 us (2%)
    pallas_call x1, Pallas kernels, body(): pl.pallas_call(kernel, out_shape=(jax.ShapeDtypeStruct((RHS, CH), BF16),...  156 us

profile of v1, /device:TPU:1, one launch (start us, length us, event | category | flops | bytes accessed | tf_op | source)
XLA Modules:
  0.0 160.2 jit_solution(13210810471434296146)
XLA Ops:
  1.3 156.0 %forward_substitution.1 = (bf16[64,256]{1,0:T(8,128)(2,1)}, f32[64,192]{1,0:T(8,128)}) custom-call(s32[126]{0:T(128)} %bitcast.17, s32[1,1]{1,0:T(1,128)S(6)} %copy.12.rows_ref, bf16[64,256]{1,0:T(8,128)(2,1)} %bitcast.14, bf16[256,256]{1,0:T(8,128)(2,1)} %bitcast.12, bf16[64,192]{1,0:T(8,128)(2,1)} %bitcast.15, bf16[256,16128]{1,0:T(8,128)(2,1)} %bitcast.9, ...), custom_call_target="tpu_custom_call" | custom-call | tf_op jit(solution)/shard_map/forward_substitution/pallas_call | solution.py:343
  157.3 1.5 copy.10
  158.8 1.4 copy.13

commit v2 on v1

--- a/solution.py
+++ b/solution.py
@@ -9,6 +9,8 @@
 
 MESH = pl.DeviceIdType.MESH
 LEVELS = 6
+TOP = LEVELS - 1
+TOP_CHUNKS = 4
 SEPS = 8
 RHS = 64
 CH = 256
@@ -38,8 +40,10 @@
     mask_ref, rows_ref, rhs_ref, inv_ref, srhs_ref, coup_hbm, dinv_hbm, scoup_hbm,
     leaf_out, sep_out,
     weights, dfull, cfull, dstack, cstack, part, core_in, xy_in, z_out, z_in, resid, sol_ref,
+    wide_in, wide_hi, wide_lo, x_all, tiles, tiles_core, tiles_xy, tiles_res, x_out, x_in,
     sem_w, sem_d, sem_c,
     zr_s, zr_r, zg_s, zg_r, xr_s, xr_r, xg_s, xg_r, cr_s, cr_r, cg_s, cg_r,
+    wz_s, wz_r, xa_s, xa_r, uc_s, uc_r, ux_s, ux_r, tg_s, tg_r, tc_s, tc_r, xo_s, xo_r,
 ):
     leaf = lax.axis_index("leaf")
     sep = lax.axis_index("sep")
@@ -130,6 +134,60 @@
         at = place(v, other if incoming else core, xy_of(v) + flip(d))
         return remote(resid.at[at], resid.at[at],
                       cg_s.at[k], cg_r.at[k], (partner, sep))
+
+    def wide(a, d, incoming=False):
+        src, first = ((cfull, first_chunk(TOP) - 1), (dfull, first_chunk(TOP)))[a]
+        to = z_peer(d)
+        cols = pl.ds(pl.multiple_of((first + to * TOP_CHUNKS) * CH, CH), TOP_CHUNKS * CH)
+        at = z_peer(SEPS - d) if incoming else sep
+        return remote(src.at[:, cols], wide_in.at[a, at],
+                      wz_s.at[a, d - 1], wz_r.at[a, d - 1], (leaf, to))
+
+    def fire(pieces):
+        for a, d in pieces:
+            wide(a, d).start()
+
+    def wide_stack(a, at, block):
+        rows = pl.ds(pl.multiple_of(at * 32, 32), 32)
+        hi, lo = split(block)
+        wide_hi[a, rows, :] = hi
+        wide_lo[a, rows, :] = lo
+
+    def wide_prep(a):
+        src, first = ((cfull, first_chunk(TOP) - 1), (dfull, first_chunk(TOP)))[a]
+        cols = pl.ds(pl.multiple_of((first + sep * TOP_CHUNKS) * CH, CH), TOP_CHUNKS * CH)
+        wide_stack(a, sep, src[:, cols])
+        for d in range(1, SEPS):
+            wide(a, d, True).wait_recv()
+            at = z_peer(SEPS - d)
+            wide_stack(a, at, wide_in[a, at])
+
+    def xa(d, incoming=False):
+        at = z_peer(SEPS - d) if incoming else sep
+        return remote(x_all.at[at], x_all.at[at], xa_s.at[d - 1], xa_r.at[d - 1],
+                      (leaf, z_peer(d)))
+
+    def uc():
+        return remote(tiles.at[other], tiles_core, uc_s.at[0], uc_r.at[0], (partner, sep))
+
+    def ux(d):
+        return remote(tiles.at[core, xy_of(TOP) + flip(d)], tiles_xy.at[d - 1],
+                      ux_s.at[d - 1], ux_r.at[d - 1], (leaf + 2 * flip(d), sep))
+
+    def tg(d, incoming=False):
+        at = xy_of(TOP) + (flip(d) if incoming else 0)
+        return remote(tiles_res.at[core, at], tiles_res.at[core, at],
+                      tg_s.at[d - 1], tg_r.at[d - 1], (leaf + 2 * flip(d), sep))
+
+    def tc(d, incoming=False):
+        which = other if incoming else core
+        at = xy_of(TOP) + flip(d)
+        return remote(tiles_res.at[which, at], tiles_res.at[which, at],
+                      tc_s.at[d], tc_r.at[d], (partner, sep))
+
+    def xo(d):
+        return remote(x_out.at[z_peer(d)], x_in.at[d - 1], xo_s.at[d - 1], xo_r.at[d - 1],
+                      (leaf, z_peer(d)))
 
     for v in range(LEVELS):
         load_w(v).start()
@@ -163,6 +221,40 @@
         t = jnp.concatenate([left, rest], axis=1)
         part[place(v, which_core, xy)] = t.reshape(SEPS, 8, CH)
 
+    def own_rows(v):
+        r = lax.broadcasted_iota(jnp.int32, (LEVELS * 32, CH), 0)
+        c = lax.broadcasted_iota(jnp.int32, (LEVELS * 32, CH), 1)
+        pick = jnp.where((r - 32 * v == c - 32 * sep) & (r >= 32 * v) & (r < 32 * v + 32), 1.0, 0.0)
+        own = jnp.dot(srhs_ref[...], pick.astype(BF16), preferred_element_type=F32)
+        return own.reshape(SEPS, 8, CH)
+
+    def tile_place(j, g):
+        return first_chunk(TOP) + (g % 2) * 2 ** (TOP - 1) + j * 4 + g // 2
+
+    def top_terms():
+        load_w(TOP).wait()
+
+        def some(at, carry):
+            for j in range(TOP_CHUNKS):
+                m = at * TOP_CHUNKS + j
+                block = 2 * (first_chunk(TOP) + m)
+                col = pl.multiple_of((first_chunk(TOP) + m) * CH, CH)
+                t = jnp.dot(sol_ref[...], weights[:, pl.ds(col, CH)], preferred_element_type=F32)
+                left = t[:, :128] * (-mask_ref[block].astype(F32))
+                rest = t[:, 128:] * (-mask_ref[block + 1].astype(F32))
+                t = jnp.concatenate([left, rest], axis=1)
+                for g in range(8):
+                    part[tile_place(j, g), at] = t[8 * g : 8 * g + 8]
+            return carry
+
+        lax.fori_loop(0, SEPS, some, 0)
+        own = own_rows(TOP)
+        at = leaf // TOP_CHUNKS
+        j = lax.rem(leaf, TOP_CHUNKS)
+        for g in range(8):
+            k = tile_place(j, g)
+            part[k, at] = part[k, at] + own[g]
+
     def terms(v):
         load_w(v).wait()
         if v == 0:
@@ -181,12 +273,8 @@
                 some(0, 0)
             else:
                 lax.fori_loop(0, n // step, some, 0)
-        r = lax.broadcasted_iota(jnp.int32, (LEVELS * 32, CH), 0)
-        c = lax.broadcasted_iota(jnp.int32, (LEVELS * 32, CH), 1)
-        pick = jnp.where((r - 32 * v == c - 32 * sep) & (r >= 32 * v) & (r < 32 * v + 32), 1.0, 0.0)
-        own = jnp.dot(srhs_ref[...], pick.astype(BF16), preferred_element_type=F32)
         at = mine(v)
-        part[at] = part[at] + own.reshape(SEPS, 8, CH)
+        part[at] = part[at] + own_rows(v)
 
     def stack(src, dst, start, size):
         cols = pl.ds(pl.multiple_of(start, CH), size)
@@ -233,7 +321,31 @@
     z_out[0] = part[0]
     pl.semaphore_wait(barrier, 1 + 15 + 7)
 
-    for v in range(LEVELS):
+    quarter = lax.broadcasted_iota(jnp.int32, (16, 128), 1) // 32
+
+    def top_xy(some):
+        for d in some:
+            i = xy_of(TOP) + flip(d)
+            cr(TOP, i).wait_recv()
+            at = place(TOP, core, i)
+            part[at] = part[at] + core_in[core_slot(TOP) + i]
+            xr(TOP, d).start()
+
+    def top_sum():
+        i = xy_of(TOP)
+        cr(TOP, i).wait_recv()
+        total = part[mine(TOP)] + core_in[core_slot(TOP) + i]
+        for d in range(1, 16):
+            xr(TOP, d).wait_recv()
+            total = total + xy_in[xy_slot(TOP) + d - 1]
+        z_out[TOP] = total
+
+    def top_rows():
+        for d in range(1, SEPS):
+            zr(TOP, d).wait_recv()
+
+    C, D = 0, 1
+    for v in range(TOP):
         if v >= 1:
             n = 2 ** (v - 1)
             step = min(n, 4)
@@ -261,6 +373,7 @@
                 at = place(v, core, i)
                 part[at] = part[at] + core_in[core_slot(v) + i]
                 xr(v, d).start()
+            fire({2: ((C, 2), (C, 6)), 3: ((C, 3), (C, 5)), 4: ((D, 3), (D, 5))}.get(v, ()))
             i = xy_of(v)
             cr(v, i).wait_recv()
             total = part[mine(v)] + core_in[core_slot(v) + i]
@@ -275,8 +388,22 @@
             terms(1)
             prep(1)
             terms(2)
-        elif v < LEVELS - 1:
-            prep(v + 1)
+        elif v == 1:
+            load_c(TOP).wait()
+            load_d(TOP).wait()
+            fire(((C, 1), (C, 7)))
+            prep(2)
+            top_terms()
+            for i in range(2 ** (TOP - 1)):
+                cr(TOP, i).start()
+        elif v == 2:
+            prep(3)
+            top_xy(range(8, 16))
+        elif v == 3:
+            prep(4)
+            top_sum()
+        else:
+            wide_prep(C)
         if v >= 1:
             for i in range(2 ** (v - 1)):
                 cr(v, i).wait_send()
@@ -289,8 +416,14 @@
         resid[mine(v), sep] = total
         for d in range(1, SEPS):
             zg(v, d).start()
-        if v + 3 < LEVELS:
-            terms(v + 3)
+        if v == 0:
+            terms(3)
+        elif v == 1:
+            fire(((D, 1), (D, 7)))
+            terms(4)
+            top_xy(range(1, 8))
+        elif v == 4:
+            top_rows()
         for d in range(1, SEPS):
             zr(v, d).wait_send()
         for d in range(1, SEPS):
@@ -299,6 +432,10 @@
             cg(v, 0).start()
             for d in peers(v):
                 xg(v, d).start()
+        if v == 3:
+            for d in range(1, SEPS):
+                zr(TOP, d).start()
+        fire({2: ((D, 2), (D, 6)), 3: ((C, 4),), 4: ((D, 4),)}.get(v, ()))
         acc = jnp.zeros((2 * RHS, 128), F32)
         if v == 0:
             acc = product(0, 0, 0, 0, acc)
@@ -315,13 +452,20 @@
                 acc = product(v, other, i, place(v, other, i), acc)
         t = acc[:RHS] + acc[RHS:]
         x = t + pltpu.roll(t, 32, 1)
+        if v == TOP - 1:
+            x_all[sep] = functools.reduce(
+                lambda kept, b: jnp.where(quarter == b, x[16 * b : 16 * b + 16], kept),
+                range(1, 4), x[:16])
+            for d in range(1, SEPS):
+                xa(d).start()
         if v < 4:
             old = jnp.zeros_like(x) if v == 0 else sep_out[:, :128]
             sep_out[:, :128] = jnp.where(lanes // 32 == v, x, old)
         else:
             sep_out[:, 32 * v : 32 * v + 32] = x[:, 32 * (v - 4) : 32 * (v - 3)]
-        hi, lo = split(x)
-        xs = jnp.where(lanes < 64, hi.astype(F32), lo.astype(F32)).astype(BF16)
+        if v < TOP - 1:
+            hi, lo = split(x)
+            xs = jnp.where(lanes < 64, hi.astype(F32), lo.astype(F32)).astype(BF16)
         for d in range(1, SEPS):
             zg(v, d).wait_send()
         if v >= 1:
@@ -329,6 +473,90 @@
                 cg(v, d).wait_send()
             for d in peers(v):
                 xg(v, d).wait_send()
+
+    for d in range(1, SEPS):
+        xa(d, True).wait_recv()
+
+    def merged(pieces):
+        return functools.reduce(
+            lambda kept, b: jnp.where(quarter == b, pieces[b], kept), range(1, 4), pieces[0])
+
+    def turned(tile, quarters):
+        shift = 32 * (quarters % 4)
+        return pltpu.roll(tile, shift, 1) if shift else tile
+
+    below = [x_all[s] for s in range(SEPS)]
+    x = jnp.concatenate([
+        jnp.concatenate([merged([turned(below[4 * h + q], q - b) for q in range(4)])
+                         for b in range(4)], axis=0)
+        for h in range(2)], axis=1)
+    hi, lo = split(x)
+    both = jnp.concatenate([hi, lo], axis=0)
+    for j in range(TOP_CHUNKS):
+        cols = slice(j * CH, j * CH + CH)
+        t = jnp.dot(both, wide_hi[C, :, cols], preferred_element_type=F32)
+        t = t[:RHS] + t[RHS:] + jnp.dot(hi, wide_lo[C, :, cols], preferred_element_type=F32)
+        for g in range(8):
+            tiles[g % 2, j * 4 + g // 2] = -t[8 * g : 8 * g + 8]
+    uc().start()
+    wide_prep(D)
+    uc().wait_recv()
+    for d in range(1, 16):
+        at = xy_of(TOP) + flip(d)
+        tiles[core, at] = tiles[core, at] + tiles_core[at]
+        ux(d).start()
+    at = xy_of(TOP)
+    total = z_out[TOP, sep] + (tiles[core, at] + tiles_core[at])
+    for d in range(1, SEPS):
+        total = total + z_in[TOP, d - 1]
+    for d in range(1, 16):
+        ux(d).wait_recv()
+        total = total + tiles_xy[d - 1]
+    tiles_res[core, at] = total
+    tc(0).start()
+    for d in range(1, 16):
+        tg(d).start()
+    for d in range(1, 16):
+        tg(d, True).wait_recv()
+        tc(d).start()
+    for d in range(16):
+        tc(d, True).wait_recv()
+    solved_top = jnp.zeros((RHS, CH), F32)
+    dims = (((1,), (1,)), ((), ()))
+    for j in range(TOP_CHUNKS):
+        cols = slice(j * CH, j * CH + CH)
+        hi, lo = split(jnp.concatenate([tiles_res[g % 2, j * 4 + g // 2] for g in range(8)], axis=0))
+        both = jnp.concatenate([hi, lo], axis=0)
+        t = lax.dot_general(both, wide_hi[D, :, cols], dims, preferred_element_type=F32)
+        solved_top = solved_top + t[:RHS] + t[RHS:] + lax.dot_general(
+            hi, wide_lo[D, :, cols], dims, preferred_element_type=F32)
+    for h in range(2):
+        rows = [solved_top[16 * b : 16 * b + 16, 128 * h : 128 * h + 128] for b in range(4)]
+        for q in range(4):
+            x_out[4 * h + q] = merged([turned(rows[b], b - q) for b in range(4)])
+    for d in range(1, SEPS):
+        xo(d).start()
+    for d in range(1, SEPS):
+        xa(d).wait_send()
+        wide(C, d).wait_send()
+        wide(D, d).wait_send()
+        zr(TOP, d).wait_send()
+    for i in range(2 ** (TOP - 1)):
+        cr(TOP, i).wait_send()
+        tc(i).wait_send()
+    uc().wait_send()
+    for d in range(1, 16):
+        xr(TOP, d).wait_send()
+        ux(d).wait_send()
+        tg(d).wait_send()
+    total = x_out[sep]
+    for d in range(1, SEPS):
+        xo(d).wait_recv()
+        total = total + x_in[d - 1]
+    for b in range(4):
+        sep_out[16 * b : 16 * b + 16, 32 * TOP : 32 * TOP + 32] = turned(total, 1 - b)[:, 32:64]
+    for d in range(1, SEPS):
+        xo(d).wait_send()
 
 
 def body(
@@ -361,10 +589,23 @@
             pltpu.VMEM((LEVELS, SEPS - 1, 8, CH), F32),
             pltpu.VMEM((63, SEPS, 8, CH), F32),
             pltpu.VMEM((RHS, CH), BF16),
+            pltpu.VMEM((2, SEPS, 32, TOP_CHUNKS * CH), F32),
+            pltpu.VMEM((2, CH, TOP_CHUNKS * CH), BF16),
+            pltpu.VMEM((2, CH, TOP_CHUNKS * CH), BF16),
+            pltpu.VMEM((SEPS, 16, 128), F32),
+            pltpu.VMEM((2, 16, 8, CH), F32),
+            pltpu.VMEM((16, 8, CH), F32),
+            pltpu.VMEM((15, 8, CH), F32),
+            pltpu.VMEM((2, 16, 8, CH), F32),
+            pltpu.VMEM((SEPS, 16, 128), F32),
+            pltpu.VMEM((SEPS - 1, 16, 128), F32),
             dma((LEVELS,)), dma((LEVELS,)), dma((LEVELS,)),
             dma((LEVELS, 7)), dma((LEVELS, 7)), dma((LEVELS, 7)), dma((LEVELS, 7)),
             dma((26,)), dma((26,)), dma((26,)), dma((26,)),
             dma((31,)), dma((31,)), dma((31,)), dma((31,)),
+            dma((2, 7)), dma((2, 7)), dma((7,)), dma((7,)), dma((1,)), dma((1,)),
+            dma((15,)), dma((15,)), dma((15,)), dma((15,)), dma((16,)), dma((16,)),
+            dma((7,)), dma((7,)),
         ],
         compiler_params=pltpu.CompilerParams(
             collective_id=0, has_side_effects=True, vmem_limit_bytes=60 * 2**20),

time: 160 us -> 145 us (0.906)
  Pallas kernels: 156 us -> 140 us
    pallas_call x1, Pallas kernels: 156 us -> 140 us  [body(): pl.pallas_call(kernel, out_shape=(jax.ShapeDtypeStruct((RHS, CH), BF16),...]
where the time goes in v2:
time: 145 us
  Pallas kernels  140 us (97%)
  local copies, waits for them, and re-layouts  2.91 us (2%)
    pallas_call x1, Pallas kernels, body(): pl.pallas_call(kernel, out_shape=(jax.ShapeDtypeStruct((RHS, CH), BF16),...  140 us
    unnamed x2, local copies, waits for them, and re-layouts  2.91 us

profile of v2, /device:TPU:1, one launch (start us, length us, event | category | flops | bytes accessed | tf_op | source)
XLA Modules:
  0.0 144.5 jit_solution(18194452889605316718)
XLA Ops:
  1.3 140.3 %forward_substitution.1 = (bf16[64,256]{1,0:T(8,128)(2,1)}, f32[64,192]{1,0:T(8,128)}) custom-call(s32[126]{0:T(128)} %bitcast.17, s32[1,1]{1,0:T(1,128)S(6)} %copy.12.rows_ref, bf16[64,256]{1,0:T(8,128)(2,1)} %bitcast.14, bf16[256,256]{1,0:T(8,128)(2,1)} %bitcast.12, bf16[64,192]{1,0:T(8,128)(2,1)} %bitcast.15, bf16[256,16128]{1,0:T(8,128)(2,1)} %bitcast.9, ...), custom_call_target="tpu_custom_call" | custom-call | tf_op jit(solution)/shard_map/forward_substitution/pallas_call | solution.py:571
  141.6 1.5 %copy.10 = f32[64,1,1,192]{3,2,1,0:T(1,128)} copy(f32[64,1,1,192]{3,0,2,1:T(8,128)} %bitcast.13) | data formatting | bytes 98304
  143.2 1.4 copy.13

commit v3 on v2

v3 whole, which is shorter than its diff:
```python
import functools

import jax
import jax.numpy as jnp
from jax import lax
from jax.experimental import pallas as pl
from jax.experimental.pallas import tpu as pltpu
from jax.sharding import PartitionSpec as P

MESH = pl.DeviceIdType.MESH
LEVELS = 6
TOP = LEVELS - 1
TOP_CHUNKS = 4
ORDER = (4, 3, 5, 2, 6, 1, 7, 0)
W_PARTS = (0, 1, 3, 5, 6)
D_PARTS = (0, 2, 5, 6)
GROUPS = ((0, 3), (3, 2), (5, 3))
SEPS = 8
RHS = 64
CH = 256
F32 = jnp.float32
BF16 = jnp.bfloat16


def first_chunk(v):
    return 2**v - 1


def xy_slot(v):
    return sum(2 ** (u - 1) - 1 for u in range(2, v))


def core_slot(v):
    return 2 ** (v - 1) - 1


def split(x):
    hi = x.astype(BF16)
    lo = (x - hi.astype(F32)).astype(BF16)
    return hi, lo


def kernel(
    mask_ref, rows_ref, rhs_ref, inv_ref, srhs_ref, coup_hbm, dinv_hbm, scoup_hbm,
    leaf_out, sep_out,
    weights, dfull, cfull, dstack, cstack, part, core_in, xy_in, z_out, z_in, resid, sol_ref,
    turn_a, turn_b, sol_rel, srhs_rel, sep_rel,
    wide_in, wide_hi, wide_lo, x_all, tiles, tiles_core, tiles_xy, tiles_res, x_out, x_in,
    sem_w, sem_d, sem_c, send, z_sem, core_sem, xr_sem, xg_sem, top_sem,
):
    leaf = lax.axis_index("leaf")
    sep = lax.axis_index("sep")
    core = lax.rem(leaf, 2)
    other = 1 - core
    bits = [lax.rem(leaf // 2 ** (k + 1), 2) for k in range(4)]
    partner = leaf + 1 - 2 * core

    def xy_of(v):
        return lax.rem(leaf // 2, 2 ** (v - 1))

    def flip(d):
        return sum(2**k * (1 - 2 * bits[k]) for k in range(4) if d >> k & 1)

    def place(v, which_core, xy):
        if v == 0:
            return 0
        return first_chunk(v) + which_core * 2 ** (v - 1) + xy

    def mine(v):
        return 0 if v == 0 else place(v, core, xy_of(v))

    def column(v, which_core, xy):
        if v == 0:
            return 0
        return pl.multiple_of((first_chunk(v) + 2 * xy + which_core) * CH, CH)

    def peers(v):
        return range(1, 2 ** (v - 1)) if v >= 2 else range(0)

    def load_w(k):
        cols = pl.ds(first_chunk(W_PARTS[k]) * CH,
                     (first_chunk(W_PARTS[k + 1]) - first_chunk(W_PARTS[k])) * CH)
        return pltpu.make_async_copy(coup_hbm.at[:, cols], weights.at[:, cols], sem_w.at[k])

    def load_d(k):
        cols = pl.ds(first_chunk(D_PARTS[k]) * CH,
                     (first_chunk(D_PARTS[k + 1]) - first_chunk(D_PARTS[k])) * CH)
        return pltpu.make_async_copy(dinv_hbm.at[:, cols], dfull.at[:, cols], sem_d.at[k])

    def load_c(k):
        start = max(first_chunk(D_PARTS[k]) - 1, 0)
        cols = pl.ds(start * CH, (first_chunk(D_PARTS[k + 1]) - 1 - start) * CH)
        return pltpu.make_async_copy(scoup_hbm.at[:, cols], cfull.at[:, cols], sem_c.at[k])

    def remote(src, dst, sent, arrived, to):
        return pltpu.make_async_remote_copy(
            src_ref=src, dst_ref=dst, send_sem=sent, recv_sem=arrived,
            device_id=to, device_id_type=MESH)

    def z_peer(d):
        return lax.rem(sep + d, SEPS)

    next_z = (leaf, z_peer(1))
    next_core = (partner, sep)
    next_xy = (leaf + 2 * flip(1), sep)

    def zr(v, d):
        top = v == TOP
        return remote(z_out.at[v, z_peer(d) if top else ORDER.index(d)], z_in.at[v, d - 1],
                      send.at[1 if top else 0], top_sem.at[0] if top else z_sem.at[0],
                      (leaf, z_peer(d)))

    def all_zr(v):
        top = v == TOP
        return remote(z_in.at[v], z_in.at[v], send.at[1 if top else 0],
                      top_sem.at[0] if top else z_sem.at[0], next_z)

    def zg(v, d):
        there = ORDER.index(SEPS - d)
        g = [first <= there < first + count for first, count in GROUPS].index(True)
        return remote(resid.at[mine(v), SEPS - 1], resid.at[mine(v), there],
                      send.at[2], z_sem.at[1 + g], (leaf, z_peer(d)))

    def all_zg(v, g):
        first, count = GROUPS[g]
        rows = resid.at[mine(v), pl.ds(first, count - (g == 2))]
        return remote(rows, rows, send.at[2], z_sem.at[1 + g], next_z)

    def all_zg_sent(v):
        return remote(z_in.at[v], z_in.at[v], send.at[2], z_sem.at[1], next_z)

    def rows_of(g):
        return pl.ds(*GROUPS[g])

    def xr(v, d, g):
        k = xy_slot(v) + d - 1
        at = place(v, core, xy_of(v) + flip(d))
        to = (leaf + 2 * flip(d), sep)
        if v == TOP:
            return remote(part.at[at], xy_in.at[k], send.at[4], top_sem.at[1], to)
        return remote(part.at[at, rows_of(g)], xy_in.at[k, rows_of(g)],
                      send.at[3], xr_sem.at[v - 2, g], to)

    def all_xr(v, g):
        slots = pl.ds(xy_slot(v), len(peers(v)))
        if v == TOP:
            ref = xy_in.at[slots]
            return remote(ref, ref, send.at[4], top_sem.at[1], next_xy)
        ref = xy_in.at[slots, rows_of(g)]
        return remote(ref, ref, send.at[3], xr_sem.at[v - 2, g], next_xy)

    def all_xr_sent(v):
        ref = xy_in.at[pl.ds(xy_slot(v), len(peers(v)))]
        return remote(ref, ref, send.at[3], xr_sem.at[v - 2, 0], next_xy)

    def xg(v, d, g):
        at = mine(v)
        return remote(resid.at[at, rows_of(g)], resid.at[at, rows_of(g)],
                      send.at[5], xg_sem.at[d - 1], (leaf + 2 * flip(d), sep))

    def all_xg(v, d):
        ref = resid.at[place(v, core, xy_of(v) + flip(d))]
        return remote(ref, ref, send.at[5], xg_sem.at[d - 1], (leaf + 2 * flip(d), sep))

    def all_xg_sent(v):
        ref = xy_in.at[pl.ds(xy_slot(v), len(peers(v)))]
        return remote(ref, ref, send.at[5], xg_sem.at[0], next_xy)

    def cr(v, i):
        top = v == TOP
        return remote(part.at[place(v, other, i)], core_in.at[core_slot(v) + i],
                      send.at[7 if top else 6], top_sem.at[2] if top else core_sem.at[0],
                      next_core)

    def all_cr(v):
        top = v == TOP
        ref = core_in.at[pl.ds(core_slot(v), 2 ** (v - 1))]
        return remote(ref, ref, send.at[7 if top else 6],
                      top_sem.at[2] if top else core_sem.at[0], next_core)

    def cg(v, d):
        ref = resid.at[place(v, core, xy_of(v) + flip(d))]
        return remote(ref, ref, send.at[8], core_sem.at[1], next_core)

    def all_cg(v):
        ref = resid.at[pl.ds(place(v, other, 0), 2 ** (v - 1))]
        return remote(ref, ref, send.at[8], core_sem.at[1], next_core)

    def wide(a, d):
        src, first = ((cfull, first_chunk(TOP) - 1), (dfull, first_chunk(TOP)))[a]
        to = z_peer(d)
        cols = pl.ds(pl.multiple_of((first + to * TOP_CHUNKS) * CH, CH), TOP_CHUNKS * CH)
        return remote(src.at[:, cols], wide_in.at[a, d - 1],
                      send.at[9], top_sem.at[3 + a], (leaf, to))

    def all_wide(a):
        return remote(wide_in.at[a], wide_in.at[a], send.at[9], top_sem.at[3 + a], next_z)

    def fire(pieces):
        for a, d in pieces:
            wide(a, d).start()

    def wide_stack(a, at, block):
        rows = pl.ds(pl.multiple_of(at * 32, 32), 32)
        hi, lo = split(block)
        wide_hi[a, rows, :] = hi
        wide_lo[a, rows, :] = lo

    def wide_prep(a):
        src, first = ((cfull, first_chunk(TOP) - 1), (dfull, first_chunk(TOP)))[a]
        cols = pl.ds(pl.multiple_of((first + sep * TOP_CHUNKS) * CH, CH), TOP_CHUNKS * CH)
        wide_stack(a, sep, src[:, cols])
        all_wide(a).wait_recv()
        for d in range(1, SEPS):
            wide_stack(a, z_peer(SEPS - d), wide_in[a, d - 1])

    def xa(d):
        return remote(x_all.at[0], x_all.at[d], send.at[10], top_sem.at[5], (leaf, z_peer(d)))

    def all_xa():
        ref = x_all.at[pl.ds(1, SEPS - 1)]
        return remote(ref, ref, send.at[10], top_sem.at[5], next_z)

    def uc():
        return remote(tiles.at[other], tiles_core, send.at[11], top_sem.at[6], next_core)

    def ux(d):
        return remote(tiles.at[core, xy_of(TOP) + flip(d)], tiles_xy.at[d - 1],
                      send.at[12], top_sem.at[7], (leaf + 2 * flip(d), sep))

    def all_ux():
        return remote(tiles_xy, tiles_xy, send.at[12], top_sem.at[7], next_xy)

    def tg(d):
        return remote(tiles_res.at[0, 0], tiles_res.at[0, d],
                      send.at[13], top_sem.at[8], (leaf + 2 * flip(d), sep))

    def all_tg():
        ref = tiles_res.at[0, pl.ds(1, 15)]
        return remote(ref, ref, send.at[13], top_sem.at[8], next_xy)

    def tc():
        return remote(tiles_res.at[0], tiles_res.at[1], send.at[14], top_sem.at[9], next_core)

    def xo(d):
        return remote(x_out.at[z_peer(d)], x_in.at[d - 1], send.at[15], top_sem.at[10],
                      (leaf, z_peer(d)))

    def all_xo():
        return remote(x_in, x_in, send.at[15], top_sem.at[10], next_z)

    barrier = pltpu.get_barrier_semaphore()
    pl.semaphore_signal(barrier, inc=1, device_id=(partner, sep), device_id_type=MESH)
    for d in range(1, 16):
        pl.semaphore_signal(
            barrier, inc=1, device_id=(leaf + 2 * flip(d), sep), device_id_type=MESH)
    for d in range(1, SEPS):
        pl.semaphore_signal(
            barrier, inc=1, device_id=(leaf, z_peer(d)), device_id_type=MESH)

    load_w(0).start()
    load_d(0).start()
    load_c(0).start()
    load_w(1).start()
    load_d(1).start()
    load_c(1).start()
    load_w(2).start()
    load_d(2).start()
    load_c(2).start()
    load_w(3).start()

    live = lax.broadcasted_iota(jnp.int32, (RHS, CH), 1) < rows_ref[0, 0]
    right = jnp.where(live, rhs_ref[...].astype(F32), 0.0).astype(BF16)
    solved = jnp.dot(right, inv_ref[...], preferred_element_type=F32)
    solved = jnp.where(live, solved, 0.0)
    sol_ref[...] = solved.astype(BF16)
    leaf_out[...] = solved.astype(BF16)

    def turned_rows(scratch, value):
        scratch[...] = value.reshape(scratch.shape)
        return jnp.concatenate([scratch[z_peer(d)] for d in ORDER], axis=0)

    sol_rel[...] = turned_rows(turn_a, solved).astype(BF16)
    srhs_rel[...] = turned_rows(turn_b, srhs_ref[...].astype(F32)).astype(BF16)

    def terms_chunk(v, which_core, xy):
        m = 0 if v == 0 else 2 * xy + which_core
        block = 2 * (first_chunk(v) + m)
        col = column(v, which_core, xy)
        t = jnp.dot(sol_rel[...], weights[:, pl.ds(col, CH)], preferred_element_type=F32)
        left = t[:, :128] * (-mask_ref[block].astype(F32))
        rest = t[:, 128:] * (-mask_ref[block + 1].astype(F32))
        t = jnp.concatenate([left, rest], axis=1)
        part[place(v, which_core, xy)] = t.reshape(SEPS, 8, CH)

    def own_rows(v, rows_ref):
        r = lax.broadcasted_iota(jnp.int32, (LEVELS * 32, CH), 0)
        c = lax.broadcasted_iota(jnp.int32, (LEVELS * 32, CH), 1)
        pick = jnp.where((r - 32 * v == c - 32 * sep) & (r >= 32 * v) & (r < 32 * v + 32), 1.0, 0.0)
        own = jnp.dot(rows_ref[...], pick.astype(BF16), preferred_element_type=F32)
        return own.reshape(SEPS, 8, CH)

    def tile_place(j, g):
        return first_chunk(TOP) + (g % 2) * 2 ** (TOP - 1) + j * 4 + g // 2

    def top_terms():
        def some(at, carry):
            for j in range(TOP_CHUNKS):
                m = at * TOP_CHUNKS + j
                block = 2 * (first_chunk(TOP) + m)
                col = pl.multiple_of((first_chunk(TOP) + m) * CH, CH)
                t = jnp.dot(sol_ref[...], weights[:, pl.ds(col, CH)], preferred_element_type=F32)
                left = t[:, :128] * (-mask_ref[block].astype(F32))
                rest = t[:, 128:] * (-mask_ref[block + 1].astype(F32))
                t = jnp.concatenate([left, rest], axis=1)
                for g in range(8):
                    part[tile_place(j, g), at] = t[8 * g : 8 * g + 8]
            return carry

        lax.fori_loop(0, SEPS, some, 0)
        own = own_rows(TOP, srhs_ref)
        at = leaf // TOP_CHUNKS
        j = lax.rem(leaf, TOP_CHUNKS)
        for g in range(8):
            k = tile_place(j, g)
            part[k, at] = part[k, at] + own[g]

    def terms(v):
        if v == 0:
            terms_chunk(0, 0, 0)
        else:
            n = 2 ** (v - 1)
            step = min(n, 2)

            def some(i, carry):
                for j in range(step):
                    for c in range(2):
                        terms_chunk(v, c, i * step + j)
                return carry

            if n == step:
                some(0, 0)
            else:
                lax.fori_loop(0, n // step, some, 0)
        at = mine(v)
        part[at] = part[at] + own_rows(v, srhs_rel)

    def stack(src, dst, start, size):
        cols = pl.ds(pl.multiple_of(start, CH), size)
        hi, lo = split(src[:, cols])
        dst[0:32, cols] = hi
        dst[32:64, cols] = lo
        dst[64:96, cols] = hi
        dst[96:128, cols] = lo

    def stack_all(src, dst, start, size):
        width = min(size, 512)
        if size == width:
            stack(src, dst, start, size)
        else:
            def some(i, carry):
                stack(src, dst, start + i * width, width)
                return carry
            lax.fori_loop(0, size // width, some, 0)

    def prep(v):
        stack_all(dfull, dstack, first_chunk(v) * CH, 2**v * CH)
        if v:
            stack_all(cfull, cstack, (first_chunk(v) - 1) * CH, 2**v * CH)

    lanes = lax.broadcasted_iota(jnp.int32, (RHS, 128), 1)

    def product(v, which_core, xy, at, acc):
        hi, lo = split(resid[at].reshape(RHS, CH))
        rows = jnp.concatenate([hi, lo], axis=0)
        col = column(v, which_core, xy)
        return acc + lax.dot_general(
            rows, dstack[:, pl.ds(col, CH)], (((1,), (1,)), ((), ())),
            preferred_element_type=F32)

    def couple_chunk(v, xs, which_core, xy):
        at = place(v, which_core, xy)
        col = (first_chunk(v) - 1 + 2 * xy + which_core) * CH
        t = jnp.dot(xs, cstack[:, pl.ds(pl.multiple_of(col, CH), CH)], preferred_element_type=F32)
        part[at] = part[at] - t.reshape(SEPS, 8, CH)

    load_w(0).wait()
    terms(0)
    z_out[0] = part[0]
    pl.semaphore_wait(barrier, 1 + 15 + 7)

    quarter = lax.broadcasted_iota(jnp.int32, (16, 128), 1) // 32

    def top_xy(some):
        for d in some:
            i = xy_of(TOP) + flip(d)
            at = place(TOP, core, i)
            part[at] = part[at] + core_in[core_slot(TOP) + i]
            xr(TOP, d, None).start()

    def top_sum():
        i = xy_of(TOP)
        all_xr(TOP, None).wait_recv()
        total = part[mine(TOP)] + core_in[core_slot(TOP) + i]
        for d in range(1, 16):
            total = total + xy_in[xy_slot(TOP) + d - 1]
        z_out[TOP] = total

    C, D = 0, 1
    for v in range(TOP):
        if v >= 1:
            n = 2 ** (v - 1)
            step = min(n, 4)

            def theirs(i, carry):
                for j in range(step):
                    couple_chunk(v, xs, other, i * step + j)
                    cr(v, i * step + j).start()
                return carry

            def ours(i, carry):
                for j in range(step):
                    couple_chunk(v, xs, core, i * step + j)
                return carry

            if n == step:
                theirs(0, 0)
                ours(0, 0)
            else:
                lax.fori_loop(0, n // step, theirs, 0)
                lax.fori_loop(0, n // step, ours, 0)
            all_cr(v).wait_recv()
            for d in peers(v):
                i = xy_of(v) + flip(d)
                at = place(v, core, i)
                part[at] = part[at] + core_in[core_slot(v) + i]
                xr(v, d, 0).start()
            for g in range(1, 3):
                for d in peers(v):
                    xr(v, d, g).start()
            fire({2: ((C, 2), (C, 6)), 3: ((C, 3), (C, 5)), 4: ((D, 3), (D, 5))}.get(v, ()))
            i = xy_of(v)
            at = mine(v)
            part[at] = part[at] + core_in[core_slot(v) + i]
            for g, (first, count) in enumerate(GROUPS):
                total = part[at, first : first + count]
                if v >= 2:
                    all_xr(v, g).wait_recv()
                for d in peers(v):
                    total = total + xy_in[xy_slot(v) + d - 1, first : first + count]
                z_out[v, first : first + count] = total
                for d in ORDER[first : first + count]:
                    if d:
                        zr(v, d).start()
        else:
            for d in range(1, SEPS):
                zr(v, d).start()
        if v == 0:
            load_d(0).wait()
            load_c(0).wait()
            prep(0)
            load_w(1).wait()
            terms(1)
            prep(1)
            terms(2)
        elif v == 1:
            load_c(2).wait()
            load_d(2).wait()
            fire(((C, 1), (C, 7)))
            load_d(1).wait()
            load_c(1).wait()
            prep(2)
            load_w(3).wait()
            top_terms()
            for i in range(2 ** (TOP - 1)):
                cr(TOP, i).start()
        elif v == 2:
            prep(3)
            top_xy(range(8, 16))
        elif v == 3:
            prep(4)
            top_sum()
        else:
            wide_prep(C)
        if v >= 1:
            all_cr(v).wait_send()
            if v >= 2:
                all_xr_sent(v).wait_send()
        total = z_out[v, SEPS - 1]
        all_zr(v).wait_recv()
        for d in range(1, SEPS):
            total = total + z_in[v, d - 1]
        resid[mine(v), SEPS - 1] = total
        for d in range(1, SEPS):
            zg(v, d).start()
        if v == 0:
            load_w(2).wait()
            terms(3)
        elif v == 1:
            fire(((D, 1), (D, 7)))
            terms(4)
            all_cr(TOP).wait_recv()
            top_xy(range(1, 8))
        elif v == 4:
            all_zr(TOP).wait_recv()
        all_zr(v).wait_send()
        for g, (first, count) in reversed(list(enumerate(GROUPS))):
            all_zg(v, g).wait_recv()
            for d in peers(v):
                xg(v, d, g).start()
        if v >= 1:
            cg(v, 0).start()
        if v == 3:
            for d in range(1, SEPS):
                zr(TOP, d).start()
        fire({2: ((D, 2), (D, 6)), 3: ((C, 4),), 4: ((D, 4),)}.get(v, ()))
        acc = jnp.zeros((2 * RHS, 128), F32)
        if v == 0:
            acc = product(0, 0, 0, 0, acc)
        else:
            acc = product(v, core, xy_of(v), mine(v), acc)
            for d in peers(v):
                all_xg(v, d).wait_recv()
                cg(v, d).start()
                i = xy_of(v) + flip(d)
                acc = product(v, core, i, place(v, core, i), acc)
            all_cg(v).wait_recv()
            for d in range(2 ** (v - 1)):
                i = xy_of(v) + flip(d)
                acc = product(v, other, i, place(v, other, i), acc)
        t = acc[:RHS] + acc[RHS:]
        x = t + pltpu.roll(t, 32, 1)
        if v == TOP - 1:
            for p, d in enumerate(ORDER):
                turn_a[z_peer(d), :, :128] = x[8 * p : 8 * p + 8]
            x = turn_a[:, :, :128].reshape(RHS, 128)
            x_all[0] = functools.reduce(
                lambda kept, b: jnp.where(quarter == b, x[16 * b : 16 * b + 16], kept),
                range(1, 4), x[:16])
            for d in range(1, SEPS):
                xa(d).start()
        if v < 4:
            old = jnp.zeros_like(x) if v == 0 else sep_rel[...]
            sep_rel[...] = jnp.where(lanes // 32 == v, x, old)
        else:
            sep_out[:, 32 * v : 32 * v + 32] = x[:, 32 * (v - 4) : 32 * (v - 3)]
        if v < TOP - 1:
            hi, lo = split(x)
            xs = jnp.where(lanes < 64, hi.astype(F32), lo.astype(F32)).astype(BF16)
        all_zg_sent(v).wait_send()
        if v >= 1:
            all_cg(v).wait_send()
        if v >= 2:
            all_xg_sent(v).wait_send()

    for p, d in enumerate(ORDER):
        rows = pl.ds(pl.multiple_of(8 * z_peer(d), 8), 8)
        sep_out[rows, :128] = sep_rel[8 * p : 8 * p + 8]

    all_xa().wait_recv()

    def merged(pieces):
        return functools.reduce(
            lambda kept, b: jnp.where(quarter == b, pieces[b], kept), range(1, 4), pieces[0])

    def turned(tile, quarters):
        shift = 32 * (quarters % 4)
        return pltpu.roll(tile, shift, 1) if shift else tile

    below = [x_all[lax.rem(sep + SEPS - s, SEPS)] for s in range(SEPS)]
    x = jnp.concatenate([
        jnp.concatenate([merged([turned(below[4 * h + q], q - b) for q in range(4)])
                         for b in range(4)], axis=0)
        for h in range(2)], axis=1)
    hi, lo = split(x)
    both = jnp.concatenate([hi, lo], axis=0)
    for j in range(TOP_CHUNKS):
        cols = slice(j * CH, j * CH + CH)
        t = jnp.dot(both, wide_hi[C, :, cols], preferred_element_type=F32)
        t = t[:RHS] + t[RHS:] + jnp.dot(hi, wide_lo[C, :, cols], preferred_element_type=F32)
        for g in range(8):
            tiles[g % 2, j * 4 + g // 2] = -t[8 * g : 8 * g + 8]
    uc().start()
    wide_prep(D)
    uc().wait_recv()
    for d in range(1, 16):
        at = xy_of(TOP) + flip(d)
        tiles[core, at] = tiles[core, at] + tiles_core[at]
        ux(d).start()
    at = xy_of(TOP)
    total = z_out[TOP, sep] + (tiles[core, at] + tiles_core[at])
    for d in range(1, SEPS):
        total = total + z_in[TOP, d - 1]
    all_ux().wait_recv()
    for d in range(1, 16):
        total = total + tiles_xy[d - 1]
    tiles_res[0, 0] = total
    for d in range(1, 16):
        tg(d).start()
    all_tg().wait_recv()
    tc().start()
    tc().wait_recv()

    def tile(j, g):
        xy = j * 4 + g // 2
        slot = sum(2**k * (1 - bits[k] if xy >> k & 1 else bits[k]) for k in range(4))
        return tiles_res[other if g % 2 else core, slot]

    solved_top = jnp.zeros((RHS, CH), F32)
    dims = (((1,), (1,)), ((), ()))
    for j in range(TOP_CHUNKS):
        cols = slice(j * CH, j * CH + CH)
        hi, lo = split(jnp.concatenate([tile(j, g) for g in range(8)], axis=0))
        both = jnp.concatenate([hi, lo], axis=0)
        t = lax.dot_general(both, wide_hi[D, :, cols], dims, preferred_element_type=F32)
        solved_top = solved_top + t[:RHS] + t[RHS:] + lax.dot_general(
            hi, wide_lo[D, :, cols], dims, preferred_element_type=F32)
    for h in range(2):
        rows = [solved_top[16 * b : 16 * b + 16, 128 * h : 128 * h + 128] for b in range(4)]
        for q in range(4):
            x_out[4 * h + q] = merged([turned(rows[b], b - q) for b in range(4)])
    for d in range(1, SEPS):
        xo(d).start()
    all_xa().wait_send()
    all_wide(C).wait_send()
    all_wide(D).wait_send()
    all_zr(TOP).wait_send()
    all_cr(TOP).wait_send()
    all_xr(TOP, None).wait_send()
    uc().wait_send()
    all_ux().wait_send()
    all_tg().wait_send()
    tc().wait_send()
    all_xo().wait_recv()
    total = x_out[sep]
    for d in range(1, SEPS):
        total = total + x_in[d - 1]
    for b in range(4):
        sep_out[16 * b : 16 * b + 16, 32 * TOP : 32 * TOP + 32] = turned(total, 1 - b)[:, 32:64]
    all_xo().wait_send()


def body(
    leaf_rhs, leaf_inv, leaf_coupling, block_mask, leaf_rows, sep_rhs, dinv_rows, sep_coupling
):
    sums = leaf_coupling.shape[3]
    parents = sep_coupling.shape[3]
    dma = pltpu.SemaphoreType.DMA
    vmem = pl.BlockSpec(memory_space=pltpu.VMEM)
    smem = pl.BlockSpec(memory_space=pltpu.SMEM)
    hbm = pl.BlockSpec(memory_space=pl.ANY)
    leaf_solution, sep_solution = pl.pallas_call(
        kernel,
        out_shape=(
            jax.ShapeDtypeStruct((RHS, CH), BF16),
            jax.ShapeDtypeStruct((RHS, LEVELS * 32), F32),
        ),
        in_specs=[smem, smem, vmem, vmem, vmem, hbm, hbm, hbm],
        out_specs=(vmem, vmem),
        scratch_shapes=[
            pltpu.VMEM((CH, sums), BF16),
            pltpu.VMEM((32, sums), F32),
            pltpu.VMEM((32, parents), F32),
            pltpu.VMEM((128, sums), BF16),
            pltpu.VMEM((128, parents), BF16),
            pltpu.VMEM((63, SEPS, 8, CH), F32),
            pltpu.VMEM((31, SEPS, 8, CH), F32),
            pltpu.VMEM((26, SEPS, 8, CH), F32),
            pltpu.VMEM((LEVELS, SEPS, 8, CH), F32),
            pltpu.VMEM((LEVELS, SEPS - 1, 8, CH), F32),
            pltpu.VMEM((63, SEPS, 8, CH), F32),
            pltpu.VMEM((RHS, CH), BF16),
            pltpu.VMEM((SEPS, 8, CH), F32),
            pltpu.VMEM((SEPS, 8, LEVELS * 32), F32),
            pltpu.VMEM((RHS, CH), BF16),
            pltpu.VMEM((RHS, LEVELS * 32), BF16),
            pltpu.VMEM((RHS, 128), F32),
            pltpu.VMEM((2, SEPS - 1, 32, TOP_CHUNKS * CH), F32),
            pltpu.VMEM((2, CH, TOP_CHUNKS * CH), BF16),
            pltpu.VMEM((2, CH, TOP_CHUNKS * CH), BF16),
            pltpu.VMEM((SEPS, 16, 128), F32),
            pltpu.VMEM((2, 16, 8, CH), F32),
            pltpu.VMEM((16, 8, CH), F32),
            pltpu.VMEM((15, 8, CH), F32),
            pltpu.VMEM((2, 16, 8, CH), F32),
            pltpu.VMEM((SEPS, 16, 128), F32),
            pltpu.VMEM((SEPS - 1, 16, 128), F32),
            dma((4,)), dma((3,)), dma((3,)), dma((16,)), dma((4,)), dma((2,)), dma((3, 3)), dma((7,)),
            dma((11,)),
        ],
        compiler_params=pltpu.CompilerParams(
            collective_id=0, has_side_effects=True, vmem_limit_bytes=60 * 2**20),
        name="forward_substitution",
    )(
        block_mask[0, 0], leaf_rows, leaf_rhs[:, 0, 0, :], leaf_inv[0, 0], sep_rhs[:, 0, 0, :],
        leaf_coupling[0, 0], dinv_rows[0, 0], sep_coupling[0, 0],
    )
    return (leaf_solution[:, None, None, :], sep_solution[:, None, None, :])


def solution(mesh):
    return jax.shard_map(
        body,
        mesh=mesh,
        in_specs=(
            P(None, "leaf", "sep", None),
            P("leaf", "sep", None, None),
            P("leaf", "sep", None, None),
            P("leaf", "sep", None),
            P("leaf", "sep"),
            P(None, "leaf", "sep", None),
            P("leaf", "sep", None, None),
            P("leaf", "sep", None, None),
        ),
        out_specs=(P(None, "leaf", "sep", None), P(None, "leaf", "sep", None)),
        check_vma=False,
    )
```

time: 145 us -> 134 us (0.924)
  Pallas kernels: 140 us -> 130 us
    pallas_call x1, Pallas kernels: 140 us -> 130 us  [body(): pl.pallas_call(kernel, out_shape=(jax.ShapeDtypeStruct((RHS, CH), BF16),...]
where the time goes in v3:
time: 134 us
  Pallas kernels  130 us (97%)
  local copies, waits for them, and re-layouts  2.91 us (2%)
    pallas_call x1, Pallas kernels, body(): pl.pallas_call(kernel, out_shape=(jax.ShapeDtypeStruct((RHS, CH), BF16),...  130 us
    unnamed x2, local copies, waits for them, and re-layouts  2.91 us

profile of v3, /device:TPU:1, one launch (start us, length us, event | category | flops | bytes accessed | tf_op | source)
XLA Modules:
  0.0 134.1 jit_solution(14808563164790524619)
XLA Ops:
  1.3 129.9 %forward_substitution.1 = (bf16[64,256]{1,0:T(8,128)(2,1)}, f32[64,192]{1,0:T(8,128)}) custom-call(s32[126]{0:T(128)} %bitcast.17, s32[1,1]{1,0:T(1,128)S(6)} %copy.12.rows_ref, bf16[64,256]{1,0:T(8,128)(2,1)} %bitcast.14, bf16[256,256]{1,0:T(8,128)(2,1)} %bitcast.12, bf16[64,192]{1,0:T(8,128)(2,1)} %bitcast.15, bf16[256,16128]{1,0:T(8,128)(2,1)} %bitcast.9, ...), custom_call_target="tpu_custom_call" | custom-call | tf_op jit(solution)/shard_map/forward_substitution/pallas_call | solution.py:652
  131.2 1.5 %copy.10 = f32[64,1,1,192]{3,2,1,0:T(1,128)} copy(f32[64,1,1,192]{3,0,2,1:T(8,128)} %bitcast.13) | data formatting | bytes 98304
  132.7 1.4 %copy.13 = bf16[64,1,1,256]{3,0,2,1:T(8,128)(2,1)} copy(bf16[64,1,1,256]{3,0,2,1:T(8,128)(2,1)} %bitcast.16) | data formatting | bytes 65536

commit v4 on v3

--- a/solution.py
+++ b/solution.py
@@ -9,13 +9,33 @@
 
 MESH = pl.DeviceIdType.MESH
 LEVELS = 6
+SEPS = 8
 TOP = LEVELS - 1
 TOP_CHUNKS = 4
 ORDER = (4, 3, 5, 2, 6, 1, 7, 0)
 W_PARTS = (0, 1, 3, 5, 6)
 D_PARTS = (0, 2, 5, 6)
+C, D = 0, 1
+
+
+def both_ways(a, d, *halves):
+    return tuple((a, e, h) for h in halves or (0, 1) for e in sorted({d, SEPS - d}))
+
+
+WIDE_COPIES = {
+    (1, "z"): both_ways(C, 1),
+    (1, "g"): both_ways(D, 1),
+    (1, "x"): both_ways(C, 2),
+    (2, "z"): both_ways(D, 2, 0),
+    (2, "g"): both_ways(D, 2, 1),
+    (2, "x"): both_ways(C, 3),
+    (3, "z"): both_ways(D, 3, 0),
+    (3, "g"): both_ways(D, 3, 1),
+    (3, "x"): both_ways(C, 4),
+    (4, "x"): both_ways(D, 4, 0),
+    (5, "x"): both_ways(D, 4, 1),
+}
 GROUPS = ((0, 3), (3, 2), (5, 3))
-SEPS = 8
 RHS = 64
 CH = 256
 F32 = jnp.float32
@@ -41,12 +61,13 @@
 
 
 def kernel(
-    mask_ref, rows_ref, rhs_ref, inv_ref, srhs_ref, coup_hbm, dinv_hbm, scoup_hbm,
+    mask_ref, rows_ref, rhs_hbm, inv_hbm, srhs_hbm, coup_hbm, dinv_hbm, scoup_hbm,
     leaf_out, sep_out,
+    rhs_ref, inv_ref, srhs_ref,
     weights, dfull, cfull, dstack, cstack, part, core_in, xy_in, z_out, z_in, resid, sol_ref,
     turn_a, turn_b, sol_rel, srhs_rel, sep_rel,
     wide_in, wide_hi, wide_lo, x_all, tiles, tiles_core, tiles_xy, tiles_res, x_out, x_in,
-    sem_w, sem_d, sem_c, send, z_sem, core_sem, xr_sem, xg_sem, top_sem,
+    sem_in, sem_w, sem_d, sem_c, send, z_sem, core_sem, xr_sem, xg_sem, top_sem,
 ):
     leaf = lax.axis_index("leaf")
     sep = lax.axis_index("sep")
@@ -186,19 +207,20 @@
         ref = resid.at[pl.ds(place(v, other, 0), 2 ** (v - 1))]
         return remote(ref, ref, send.at[8], core_sem.at[1], next_core)
 
-    def wide(a, d):
+    def wide(a, d, half):
         src, first = ((cfull, first_chunk(TOP) - 1), (dfull, first_chunk(TOP)))[a]
         to = z_peer(d)
-        cols = pl.ds(pl.multiple_of((first + to * TOP_CHUNKS) * CH, CH), TOP_CHUNKS * CH)
-        return remote(src.at[:, cols], wide_in.at[a, d - 1],
+        size = TOP_CHUNKS * CH // 2
+        cols = pl.ds(pl.multiple_of((first + to * TOP_CHUNKS) * CH + half * size, CH), size)
+        return remote(src.at[:, cols], wide_in.at[a, d - 1, :, pl.ds(half * size, size)],
                       send.at[9], top_sem.at[3 + a], (leaf, to))
 
     def all_wide(a):
         return remote(wide_in.at[a], wide_in.at[a], send.at[9], top_sem.at[3 + a], next_z)
 
-    def fire(pieces):
-        for a, d in pieces:
-            wide(a, d).start()
+    def fire(v, point):
+        for piece in WIDE_COPIES.get((v, point), ()):
+            wide(*piece).start()
 
     def wide_stack(a, at, block):
         rows = pl.ds(pl.multiple_of(at * 32, 32), 32)
@@ -258,6 +280,12 @@
         pl.semaphore_signal(
             barrier, inc=1, device_id=(leaf, z_peer(d)), device_id_type=MESH)
 
+    inputs = [
+        pltpu.make_async_copy(src, dst, sem_in.at[k])
+        for k, (src, dst) in enumerate(
+            [(inv_hbm, inv_ref), (rhs_hbm, rhs_ref), (srhs_hbm, srhs_ref)])]
+    for copy in inputs:
+        copy.start()
     load_w(0).start()
     load_d(0).start()
     load_c(0).start()
@@ -269,12 +297,15 @@
     load_c(2).start()
     load_w(3).start()
 
+    for copy in inputs:
+        copy.wait()
     live = lax.broadcasted_iota(jnp.int32, (RHS, CH), 1) < rows_ref[0, 0]
     right = jnp.where(live, rhs_ref[...].astype(F32), 0.0).astype(BF16)
     solved = jnp.dot(right, inv_ref[...], preferred_element_type=F32)
     solved = jnp.where(live, solved, 0.0)
     sol_ref[...] = solved.astype(BF16)
-    leaf_out[...] = solved.astype(BF16)
+    leaf_copy = pltpu.make_async_copy(sol_ref, leaf_out, sem_in.at[3])
+    leaf_copy.start()
 
     def turned_rows(scratch, value):
         scratch[...] = value.reshape(scratch.shape)
@@ -406,7 +437,13 @@
             total = total + xy_in[xy_slot(TOP) + d - 1]
         z_out[TOP] = total
 
-    C, D = 0, 1
+    def spread_sent(v):
+        all_zg_sent(v).wait_send()
+        if v >= 1:
+            all_cg(v).wait_send()
+        if v >= 2:
+            all_xg_sent(v).wait_send()
+
     for v in range(TOP):
         if v >= 1:
             n = 2 ** (v - 1)
@@ -438,7 +475,6 @@
             for g in range(1, 3):
                 for d in peers(v):
                     xr(v, d, g).start()
-            fire({2: ((C, 2), (C, 6)), 3: ((C, 3), (C, 5)), 4: ((D, 3), (D, 5))}.get(v, ()))
             i = xy_of(v)
             at = mine(v)
             part[at] = part[at] + core_in[core_slot(v) + i]
@@ -453,7 +489,7 @@
                     if d:
                         zr(v, d).start()
         else:
-            for d in range(1, SEPS):
+            for d in ORDER[:-1]:
                 zr(v, d).start()
         if v == 0:
             load_d(0).wait()
@@ -466,9 +502,9 @@
         elif v == 1:
             load_c(2).wait()
             load_d(2).wait()
-            fire(((C, 1), (C, 7)))
             load_d(1).wait()
             load_c(1).wait()
+            fire(v, "z")
             prep(2)
             load_w(3).wait()
             top_terms()
@@ -476,13 +512,16 @@
                 cr(TOP, i).start()
         elif v == 2:
             prep(3)
+            fire(v, "z")
             top_xy(range(8, 16))
         elif v == 3:
+            fire(v, "z")
             prep(4)
             top_sum()
         else:
-            wide_prep(C)
+            fire(v, "z")
         if v >= 1:
+            spread_sent(v - 1)
             all_cr(v).wait_send()
             if v >= 2:
                 all_xr_sent(v).wait_send()
@@ -491,13 +530,13 @@
         for d in range(1, SEPS):
             total = total + z_in[v, d - 1]
         resid[mine(v), SEPS - 1] = total
-        for d in range(1, SEPS):
+        for d in ORDER[:-1]:
             zg(v, d).start()
+        fire(v, "g")
         if v == 0:
             load_w(2).wait()
             terms(3)
         elif v == 1:
-            fire(((D, 1), (D, 7)))
             terms(4)
             all_cr(TOP).wait_recv()
             top_xy(range(1, 8))
@@ -513,7 +552,9 @@
         if v == 3:
             for d in range(1, SEPS):
                 zr(TOP, d).start()
-        fire({2: ((D, 2), (D, 6)), 3: ((C, 4),), 4: ((D, 4),)}.get(v, ()))
+        fire(v, "x")
+        if v == 4:
+            wide_prep(C)
         acc = jnp.zeros((2 * RHS, 128), F32)
         if v == 0:
             acc = product(0, 0, 0, 0, acc)
@@ -537,7 +578,7 @@
             x_all[0] = functools.reduce(
                 lambda kept, b: jnp.where(quarter == b, x[16 * b : 16 * b + 16], kept),
                 range(1, 4), x[:16])
-            for d in range(1, SEPS):
+            for d in ORDER[:-1]:
                 xa(d).start()
         if v < 4:
             old = jnp.zeros_like(x) if v == 0 else sep_rel[...]
@@ -547,17 +588,13 @@
         if v < TOP - 1:
             hi, lo = split(x)
             xs = jnp.where(lanes < 64, hi.astype(F32), lo.astype(F32)).astype(BF16)
-        all_zg_sent(v).wait_send()
-        if v >= 1:
-            all_cg(v).wait_send()
-        if v >= 2:
-            all_xg_sent(v).wait_send()
 
     for p, d in enumerate(ORDER):
         rows = pl.ds(pl.multiple_of(8 * z_peer(d), 8), 8)
         sep_out[rows, :128] = sep_rel[8 * p : 8 * p + 8]
 
     all_xa().wait_recv()
+    fire(TOP, "x")
 
     def merged(pieces):
         return functools.reduce(
@@ -581,7 +618,6 @@
         for g in range(8):
             tiles[g % 2, j * 4 + g // 2] = -t[8 * g : 8 * g + 8]
     uc().start()
-    wide_prep(D)
     uc().wait_recv()
     for d in range(1, 16):
         at = xy_of(TOP) + flip(d)
@@ -597,6 +633,7 @@
     tiles_res[0, 0] = total
     for d in range(1, 16):
         tg(d).start()
+    wide_prep(D)
     all_tg().wait_recv()
     tc().start()
     tc().wait_recv()
@@ -619,8 +656,9 @@
         rows = [solved_top[16 * b : 16 * b + 16, 128 * h : 128 * h + 128] for b in range(4)]
         for q in range(4):
             x_out[4 * h + q] = merged([turned(rows[b], b - q) for b in range(4)])
-    for d in range(1, SEPS):
+    for d in ORDER[:-1]:
         xo(d).start()
+    spread_sent(TOP - 1)
     all_xa().wait_send()
     all_wide(C).wait_send()
     all_wide(D).wait_send()
@@ -638,6 +676,7 @@
     for b in range(4):
         sep_out[16 * b : 16 * b + 16, 32 * TOP : 32 * TOP + 32] = turned(total, 1 - b)[:, 32:64]
     all_xo().wait_send()
+    leaf_copy.wait()
 
 
 def body(
@@ -655,9 +694,12 @@
             jax.ShapeDtypeStruct((RHS, CH), BF16),
             jax.ShapeDtypeStruct((RHS, LEVELS * 32), F32),
         ),
-        in_specs=[smem, smem, vmem, vmem, vmem, hbm, hbm, hbm],
-        out_specs=(vmem, vmem),
+        in_specs=[smem, smem, hbm, hbm, hbm, hbm, hbm, hbm],
+        out_specs=(hbm, vmem),
         scratch_shapes=[
+            pltpu.VMEM((RHS, CH), BF16),
+            pltpu.VMEM((CH, CH), BF16),
+            pltpu.VMEM((RHS, LEVELS * 32), BF16),
             pltpu.VMEM((CH, sums), BF16),
             pltpu.VMEM((32, sums), F32),
             pltpu.VMEM((32, parents), F32),
@@ -685,7 +727,7 @@
             pltpu.VMEM((2, 16, 8, CH), F32),
             pltpu.VMEM((SEPS, 16, 128), F32),
             pltpu.VMEM((SEPS - 1, 16, 128), F32),
-            dma((4,)), dma((3,)), dma((3,)), dma((16,)), dma((4,)), dma((2,)), dma((3, 3)), dma((7,)),
+            dma((4,)), dma((4,)), dma((3,)), dma((3,)), dma((16,)), dma((4,)), dma((2,)), dma((3, 3)), dma((7,)),
             dma((11,)),
         ],
         compiler_params=pltpu.CompilerParams(

time: 134 us -> 128 us (0.955)
  Pallas kernels: 130 us -> 123 us
    pallas_call x1, Pallas kernels: 130 us -> 123 us  [body(): pl.pallas_call(kernel, out_shape=(jax.ShapeDtypeStruct((RHS, CH), BF16),...]
where the time goes in v4:
time: 128 us
  Pallas kernels  123 us (96%)
  local copies, waits for them, and re-layouts  2.91 us (2%)
  between operations  1.29 us (1%)
    pallas_call x1, Pallas kernels, body(): pl.pallas_call(kernel, out_shape=(jax.ShapeDtypeStruct((RHS, CH), BF16),...  123 us
    unnamed x2, local copies, waits for them, and re-layouts  2.91 us

profile of v4, /device:TPU:1, one launch (start us, length us, event | category | flops | bytes accessed | tf_op | source)
XLA Modules:
  0.0 127.6 jit_solution(2124371241642370757)
XLA Ops:
  1.3 123.4 %forward_substitution.1 = (bf16[64,256]{1,0:T(8,128)(2,1)}, f32[64,192]{1,0:T(8,128)}) custom-call(s32[126]{0:T(128)} %bitcast.17, s32[1,1]{1,0:T(1,128)S(6)} %copy.12.rows_ref, bf16[64,256]{1,0:T(8,128)(2,1)} %bitcast.14, bf16[256,256]{1,0:T(8,128)(2,1)} %bitcast.12, bf16[64,192]{1,0:T(8,128)(2,1)} %bitcast.15, bf16[256,16128]{1,0:T(8,128)(2,1)} %bitcast.9, ...), custom_call_target="tpu_custom_call" | custom-call | tf_op jit(solution)/shard_map/forward_substitution/pallas_call | solution.py:691
  124.6 1.5 %copy.10 = f32[64,1,1,192]{3,2,1,0:T(1,128)} copy(f32[64,1,1,192]{3,0,2,1:T(8,128)} %bitcast.13) | data formatting | bytes 98304
  126.2 1.4 %copy.13 = bf16[64,1,1,256]{3,0,2,1:T(8,128)(2,1)} copy(bf16[64,1,1,256]{3,0,2,1:T(8,128)(2,1)} %bitcast.16) | data formatting | bytes 65536

commit v5 on v4

--- a/solution.py
+++ b/solution.py
@@ -27,13 +27,11 @@
     (1, "g"): both_ways(D, 1),
     (1, "x"): both_ways(C, 2),
     (2, "z"): both_ways(D, 2, 0),
-    (2, "g"): both_ways(D, 2, 1),
     (2, "x"): both_ways(C, 3),
-    (3, "z"): both_ways(D, 3, 0),
-    (3, "g"): both_ways(D, 3, 1),
+    (3, "z"): both_ways(D, 2, 1),
     (3, "x"): both_ways(C, 4),
-    (4, "x"): both_ways(D, 4, 0),
-    (5, "x"): both_ways(D, 4, 1),
+    (4, "x"): both_ways(D, 4),
+    (5, "x"): both_ways(D, 3),
 }
 GROUPS = ((0, 3), (3, 2), (5, 3))
 RHS = 64
@@ -272,14 +270,13 @@
         return remote(x_in, x_in, send.at[15], top_sem.at[10], next_z)
 
     barrier = pltpu.get_barrier_semaphore()
-    pl.semaphore_signal(barrier, inc=1, device_id=(partner, sep), device_id_type=MESH)
-    for d in range(1, 16):
+    for d in ORDER[:-1]:
+        pl.semaphore_signal(
+            barrier, inc=1, device_id=(leaf, z_peer(d)), device_id_type=MESH)
+    for d in reversed(range(1, 16)):
         pl.semaphore_signal(
             barrier, inc=1, device_id=(leaf + 2 * flip(d), sep), device_id_type=MESH)
-    for d in range(1, SEPS):
-        pl.semaphore_signal(
-            barrier, inc=1, device_id=(leaf, z_peer(d)), device_id_type=MESH)
-
+    pl.semaphore_signal(barrier, inc=1, device_id=(partner, sep), device_id_type=MESH)
     inputs = [
         pltpu.make_async_copy(src, dst, sem_in.at[k])
         for k, (src, dst) in enumerate(
@@ -594,7 +591,6 @@
         sep_out[rows, :128] = sep_rel[8 * p : 8 * p + 8]
 
     all_xa().wait_recv()
-    fire(TOP, "x")
 
     def merged(pieces):
         return functools.reduce(
@@ -618,6 +614,7 @@
         for g in range(8):
             tiles[g % 2, j * 4 + g // 2] = -t[8 * g : 8 * g + 8]
     uc().start()
+    fire(TOP, "x")
     uc().wait_recv()
     for d in range(1, 16):
         at = xy_of(TOP) + flip(d)

time: 128 us -> 125 us (0.977)
  Pallas kernels: 123 us -> 121 us
    pallas_call x1, Pallas kernels: 123 us -> 121 us  [body(): pl.pallas_call(kernel, out_shape=(jax.ShapeDtypeStruct((RHS, CH), BF16),...]
where the time goes in v5:
time: 125 us
  Pallas kernels  121 us (97%)
  local copies, waits for them, and re-layouts  2.91 us (2%)
  between operations  1.29 us (1%)
    pallas_call x1, Pallas kernels, body(): pl.pallas_call(kernel, out_shape=(jax.ShapeDtypeStruct((RHS, CH), BF16),...  121 us
    unnamed x2, local copies, waits for them, and re-layouts  2.91 us

profile of v5, /device:TPU:1, one launch (start us, length us, event | category | flops | bytes accessed | tf_op | source)
XLA Modules:
  0.0 125.0 jit_solution(5292155493772210872)
XLA Ops:
  1.3 120.8 %forward_substitution.1 = (bf16[64,256]{1,0:T(8,128)(2,1)}, f32[64,192]{1,0:T(8,128)}) custom-call(s32[126]{0:T(128)} %bitcast.17, s32[1,1]{1,0:T(1,128)S(6)} %copy.12.rows_ref, bf16[64,256]{1,0:T(8,128)(2,1)} %bitcast.14, bf16[256,256]{1,0:T(8,128)(2,1)} %bitcast.12, bf16[64,192]{1,0:T(8,128)(2,1)} %bitcast.15, bf16[256,16128]{1,0:T(8,128)(2,1)} %bitcast.9, ...), custom_call_target="tpu_custom_call" | custom-call | tf_op jit(solution)/shard_map/forward_substitution/pallas_call | solution.py:688
  122.1 1.5 %copy.10 = f32[64,1,1,192]{3,2,1,0:T(1,128)} copy(f32[64,1,1,192]{3,0,2,1:T(8,128)} %bitcast.13) | data formatting | bytes 98304
  123.7 1.4 %copy.13 = bf16[64,1,1,256]{3,0,2,1:T(8,128)(2,1)} copy(bf16[64,1,1,256]{3,0,2,1:T(8,128)(2,1)} %bitcast.16) | data formatting | bytes 65536

commit v6 on v5

--- a/solution.py
+++ b/solution.py
@@ -19,7 +19,7 @@
 
 
 def both_ways(a, d, *halves):
-    return tuple((a, e, h) for h in halves or (0, 1) for e in sorted({d, SEPS - d}))
+    return tuple((a, e, h) for h in halves or (None,) for e in sorted({d, SEPS - d}))
 
 
 WIDE_COPIES = {
@@ -208,7 +208,8 @@
     def wide(a, d, half):
         src, first = ((cfull, first_chunk(TOP) - 1), (dfull, first_chunk(TOP)))[a]
         to = z_peer(d)
-        size = TOP_CHUNKS * CH // 2
+        size = TOP_CHUNKS * CH // (1 if half is None else 2)
+        half = half or 0
         cols = pl.ds(pl.multiple_of((first + to * TOP_CHUNKS) * CH + half * size, CH), size)
         return remote(src.at[:, cols], wide_in.at[a, d - 1, :, pl.ds(half * size, size)],
                       send.at[9], top_sem.at[3 + a], (leaf, to))
@@ -243,6 +244,11 @@
 
     def uc():
         return remote(tiles.at[other], tiles_core, send.at[11], top_sem.at[6], next_core)
+
+    def uc_part(j):
+        some = pl.ds(4 * j, 4)
+        return remote(tiles.at[other, some], tiles_core.at[some],
+                      send.at[11], top_sem.at[6], next_core)
 
     def ux(d):
         return remote(tiles.at[core, xy_of(TOP) + flip(d)], tiles_xy.at[d - 1],
@@ -613,7 +619,7 @@
         t = t[:RHS] + t[RHS:] + jnp.dot(hi, wide_lo[C, :, cols], preferred_element_type=F32)
         for g in range(8):
             tiles[g % 2, j * 4 + g // 2] = -t[8 * g : 8 * g + 8]
-    uc().start()
+        uc_part(j).start()
     fire(TOP, "x")
     uc().wait_recv()
     for d in range(1, 16):

time: 125 us -> 126 us (level)
  no operation moved by 1% of the time
where the time goes in v6:
time: 126 us
  Pallas kernels  121 us (96%)
  local copies, waits for them, and re-layouts  2.91 us (2%)
  between operations  1.29 us (1%)
    pallas_call x1, Pallas kernels, body(): pl.pallas_call(kernel, out_shape=(jax.ShapeDtypeStruct((RHS, CH), BF16),...  121 us
    unnamed x2, local copies, waits for them, and re-layouts  2.91 us

profile of v6, /device:TPU:1, one launch (start us, length us, event | category | flops | bytes accessed | tf_op | source)
XLA Modules:
  0.0 125.7 jit_solution(11497771361729693706)
XLA Ops:
  1.3 121.5 %forward_substitution.1 = (bf16[64,256]{1,0:T(8,128)(2,1)}, f32[64,192]{1,0:T(8,128)}) custom-call(s32[126]{0:T(128)} %bitcast.17, s32[1,1]{1,0:T(1,128)S(6)} %copy.12.rows_ref, bf16[64,256]{1,0:T(8,128)(2,1)} %bitcast.14, bf16[256,256]{1,0:T(8,128)(2,1)} %bitcast.12, bf16[64,192]{1,0:T(8,128)(2,1)} %bitcast.15, bf16[256,16128]{1,0:T(8,128)(2,1)} %bitcast.9, ...), custom_call_target="tpu_custom_call" | custom-call | tf_op jit(solution)/shard_map/forward_substitution/pallas_call | solution.py:694
  122.8 1.5 %copy.10 = f32[64,1,1,192]{3,2,1,0:T(1,128)} copy(f32[64,1,1,192]{3,0,2,1:T(8,128)} %bitcast.13) | data formatting | bytes 98304
  124.3 1.4 %copy.13 = bf16[64,1,1,256]{3,0,2,1:T(8,128)(2,1)} copy(bf16[64,1,1,256]{3,0,2,1:T(8,128)(2,1)} %bitcast.16) | data formatting | bytes 65536
